TPU v7x, 32 devices: a whole 2x2x4 slice. The times are simulated.
32 devices in a mesh: dp: 8 (over z, x), tensor: 4 (over y, core).
Axes of the slice: x: 2, y: 2, z: 4, core: 2. Of those that a mesh axis runs over, the one named last changes fastest.
Arguments:
- tokens: bfloat16 [4096, 1024], P(('dp', 'tensor')), may hold values from -6 to 6
- lengths: int32 [8, 2], P('dp'), may hold values from 1 to 448, as said below
- cotangent: bfloat16 [4096, 1024], P(('dp', 'tensor')), may hold values from -6 to 6
- norm_gain: bfloat16 [1024], P('dp'), may hold values from 0.5 to 1.5
- query_weight: bfloat16 [1024, 1024], P('dp', 'tensor'), may hold values from -0.1875 to 0.1875
- key_weight: bfloat16 [1024, 1024], P('dp', 'tensor'), may hold values from -0.1875 to 0.1875
- value_weight: bfloat16 [1024, 2048], P('dp', 'tensor'), may hold values from -0.1875 to 0.1875
- gate_weight: bfloat16 [1024, 2048], P('dp', 'tensor'), may hold values from -0.1875 to 0.1875
- beta_weight: bfloat16 [1024, 4], P('dp', 'tensor'), may hold values from -0.1875 to 0.1875
- decay_weight: bfloat16 [1024, 4], P('dp', 'tensor'), may hold values from -0.1875 to 0.1875
- query_conv: bfloat16 [4, 1024], P(None, ('tensor', 'dp')), may hold values from -2.5 to 2.5
- key_conv: bfloat16 [4, 1024], P(None, ('tensor', 'dp')), may hold values from -2.5 to 2.5
- value_conv: bfloat16 [4, 2048], P(None, ('tensor', 'dp')), may hold values from -2.5 to 2.5
- decay_params: float32 [2, 4], P(None, 'tensor'), may hold values from -4 to 0
- head_gain: bfloat16 [2048], P(('tensor', 'dp')), may hold values from 0.5 to 1.5
- out_weight: bfloat16 [2048, 1024], P('tensor', 'dp'), may hold values from -0.1875 to 0.1875
- ffn_gain: bfloat16 [1024], P('dp'), may hold values from 0.5 to 1.5
- ffn_gate: bfloat16 [1024, 2816], P('dp', 'tensor'), may hold values from -0.1875 to 0.1875
- ffn_up: bfloat16 [1024, 2816], P('dp', 'tensor'), may hold values from -0.1875 to 0.1875
- ffn_down: bfloat16 [2816, 1024], P('tensor', 'dp'), may hold values from -0.15625 to 0.15625
Outputs:
- block_out: bfloat16 [4096, 1024], P(('dp', 'tensor'))
- tokens_grad: float32 [4096, 1024], P(('dp', 'tensor'))
- norm_gain_grad: float32 [1024], P('dp')
- query_weight_grad: float32 [1024, 1024], P('dp', 'tensor')
- key_weight_grad: float32 [1024, 1024], P('dp', 'tensor')
- value_weight_grad: float32 [1024, 2048], P('dp', 'tensor')
- gate_weight_grad: float32 [1024, 2048], P('dp', 'tensor')
- beta_weight_grad: float32 [1024, 4], P('dp', 'tensor')
- decay_weight_grad: float32 [1024, 4], P('dp', 'tensor')
- query_conv_grad: float32 [4, 1024], P(None, ('tensor', 'dp'))
- key_conv_grad: float32 [4, 1024], P(None, ('tensor', 'dp'))
- value_conv_grad: float32 [4, 2048], P(None, ('tensor', 'dp'))
- decay_params_grad: float32 [2, 4], P(None, 'tensor')
- head_gain_grad: float32 [2048], P(('tensor', 'dp'))
- out_weight_grad: float32 [2048, 1024], P('tensor', 'dp')
- ffn_gain_grad: float32 [1024], P('dp')
- ffn_gate_grad: float32 [1024, 2816], P('dp', 'tensor')
- ffn_up_grad: float32 [1024, 2816], P('dp', 'tensor')
- ffn_down_grad: float32 [2816, 1024], P('tensor', 'dp')
Inputs may be any that keep to these rules, and one draw needn't show every extreme that they name: `lengths`: each group holds two sequences; one fills 8 - 1 blocks after padding, the other one block, in either order; group 0's longer sequence has no padding.
All inputs are finite; a program needn't handle non-finite values.
Results may differ from a plain program's by a relative error of at most 0.014.
Values may be sent and summed in bfloat16 or wider, within the bound.
No kernel may reach another device: no remote copies, remote signals or barrier semaphores. Data moves between devices by JAX's collectives and lax.ppermute only.
A program may use at most 128 MiB of HBM per device.

v0:
```python
import jax
import jax.numpy as jnp
from jax import lax
from jax.sharding import PartitionSpec as P

H = 4
DK = 256
DV = 512
BLOCK = 64


HIGHEST = lax.Precision.HIGHEST


def round_trip(value):
    return lax.optimization_barrier(value.astype(jnp.bfloat16)).astype(jnp.float32)


def plain_scale(value, gain):
    return value * lax.rsqrt(jnp.mean(value * value, axis=-1, keepdims=True) + 1e-06) * gain


def plain_product(left, right):
    return jnp.dot(left, right, preferred_element_type=jnp.float32)


def transposed_product(left, right):
    return lax.dot_general(
        left, right, (((0,), (0,)), ((), ())), preferred_element_type=jnp.float32
    )


def product_back(grad, weight):
    return lax.dot_general(
        grad, weight, (((1,), (1,)), ((), ())), preferred_element_type=jnp.float32
    )


def group_layout(lengths_row, total, dtype):
    first_len = lengths_row[0]
    second_len = lengths_row[1]
    start = (first_len + BLOCK - 1) // BLOCK * BLOCK
    place = jnp.arange(total, dtype=jnp.int32)
    later = place >= start
    segment = later.astype(jnp.int32)
    valid = jnp.where(later, place - start < second_len, place < first_len).astype(dtype)
    block_starts = jnp.arange(total // BLOCK, dtype=jnp.int32) * BLOCK
    reset = ((block_starts == 0) | (block_starts == start)).astype(dtype)
    return (segment, valid, reset)


def causal_conv(proj, taps, segment):
    total = proj.shape[0]
    result = proj * taps[0]
    for offset in range(1, taps.shape[0]):
        shifted = jnp.concatenate(
            [jnp.zeros((offset, proj.shape[1]), proj.dtype), proj[: total - offset]], axis=0
        )
        same = jnp.concatenate(
            [jnp.zeros((offset,), jnp.bool_), segment[offset:] == segment[: total - offset]]
        )
        result = result + jnp.where(same[:, None], shifted, 0.0) * taps[offset]
    return result


def block_step(state, items):
    query, key, value, beta, logdecay, reset = items
    state = state * (1.0 - reset)
    size = query.shape[0]
    rows = lax.broadcasted_iota(jnp.int32, (size, size), 0)
    cols = lax.broadcasted_iota(jnp.int32, (size, size), 1)
    causal = rows >= cols
    strict = rows > cols
    running = jnp.cumsum(logdecay, axis=0)
    spread = running.T[:, :, None] - running.T[:, None, :]
    ratio = jnp.where(causal, jnp.exp(jnp.where(causal, spread, 0.0)), 0.0)
    intersection = jnp.einsum("ihd,jhd->hij", key, key, precision=HIGHEST)
    coupling = jnp.where(strict, beta.T[:, :, None] * intersection * ratio, 0.0)
    system = coupling + jnp.eye(size, dtype=coupling.dtype)[None, :, :]
    growth = jnp.exp(running)
    right = jnp.concatenate([beta[:, :, None] * value, (beta * growth)[:, :, None] * key], axis=2)
    right_heads = jnp.transpose(right, (1, 0, 2))
    solved_heads = lax.linalg.triangular_solve(
        system, right_heads, left_side=True, lower=True, unit_diagonal=True
    )
    solved = jnp.transpose(solved_heads, (1, 0, 2))
    width = value.shape[2]
    fresh = solved[:, :, :width] - jnp.einsum(
        "ihd,hde->ihe", solved[:, :, width:], state, precision=HIGHEST
    )
    scores = jnp.einsum("ihd,jhd->hij", query, key, precision=HIGHEST) * ratio
    output = jnp.einsum("ihd,hde->ihe", query * growth[:, :, None], state, precision=HIGHEST)
    output = output + jnp.einsum("hij,jhe->ihe", scores, fresh, precision=HIGHEST)
    final = running[-1]
    tail = jnp.exp(final[None, :] - running)
    state = jnp.exp(final)[:, None, None] * state + jnp.einsum(
        "jhd,jhe->hde", key * tail[:, :, None], fresh, precision=HIGHEST
    )
    return (state, output)


def mixer_front(query_proj, key_proj, value_proj, query_conv, key_conv, value_conv, segment):
    total = query_proj.shape[0]
    heads = query_proj.shape[1] // DK
    query = jax.nn.silu(causal_conv(query_proj, query_conv, segment)).reshape(total, heads, DK)
    key = jax.nn.silu(causal_conv(key_proj, key_conv, segment)).reshape(total, heads, DK)
    value = jax.nn.silu(causal_conv(value_proj, value_conv, segment)).reshape(total, heads, DV)
    query = query * lax.rsqrt(jnp.sum(query * query, axis=2, keepdims=True) + 1e-06) * DK ** (-0.5)
    key = key * lax.rsqrt(jnp.sum(key * key, axis=2, keepdims=True) + 1e-06)
    return (query, key, value)


def mixer_rest(
    query, key, value, gate_proj, beta_proj, decay_proj, decay_params, head_gain, valid, reset
):
    total = query.shape[0]
    heads = beta_proj.shape[1]
    beta = jax.nn.sigmoid(beta_proj)
    logdecay = -jnp.exp(decay_params[0]) * jax.nn.softplus(decay_proj + decay_params[1])
    blocks = total // BLOCK

    def into_blocks(piece):
        return piece.reshape((blocks, BLOCK) + piece.shape[1:])

    start_state = jnp.zeros((heads, DK, DV), jnp.float32)
    carried, mixed = lax.scan(
        block_step,
        start_state,
        (
            into_blocks(query),
            into_blocks(key),
            into_blocks(value),
            into_blocks(beta),
            into_blocks(logdecay),
            reset,
        ),
    )
    mixed = mixed.reshape(total, heads, DV) * valid[:, None, None]
    normed = (
        mixed
        * lax.rsqrt(jnp.mean(mixed * mixed, axis=2, keepdims=True) + 1e-06)
        * head_gain.reshape(heads, DV)
    )
    return normed.reshape(total, heads * DV) * jax.nn.silu(gate_proj)


def local(
    tokens,
    lengths,
    cotangent,
    norm_gain,
    query_weight,
    key_weight,
    value_weight,
    gate_weight,
    beta_weight,
    decay_weight,
    query_conv,
    key_conv,
    value_conv,
    decay_params,
    head_gain,
    out_weight,
    ffn_gain,
    ffn_gate,
    ffn_up,
    ffn_down,
):
    (
        norm_whole,
        query_whole,
        key_whole,
        value_whole,
        gate_whole,
        beta_whole,
        decay_whole,
        query_taps,
        key_taps,
        value_taps,
        head_whole,
        out_whole,
        ffn_gain_whole,
        gate_ffn_whole,
        up_ffn_whole,
        down_ffn_whole,
    ) = (
        lax.all_gather(norm_gain, "dp", axis=0, tiled=True),
        lax.all_gather(query_weight, "dp", axis=0, tiled=True),
        lax.all_gather(key_weight, "dp", axis=0, tiled=True),
        lax.all_gather(value_weight, "dp", axis=0, tiled=True),
        lax.all_gather(gate_weight, "dp", axis=0, tiled=True),
        lax.all_gather(beta_weight, "dp", axis=0, tiled=True),
        lax.all_gather(decay_weight, "dp", axis=0, tiled=True),
        lax.all_gather(query_conv, "dp", axis=1, tiled=True),
        lax.all_gather(key_conv, "dp", axis=1, tiled=True),
        lax.all_gather(value_conv, "dp", axis=1, tiled=True),
        lax.all_gather(head_gain, "dp", axis=0, tiled=True),
        lax.all_gather(out_weight, "dp", axis=1, tiled=True),
        lax.all_gather(ffn_gain, "dp", axis=0, tiled=True),
        lax.all_gather(ffn_gate, "dp", axis=0, tiled=True),
        lax.all_gather(ffn_up, "dp", axis=0, tiled=True),
        lax.all_gather(ffn_down, "dp", axis=1, tiled=True),
    )
    token_rows = tokens.astype(jnp.float32)
    first_norm, first_pull = jax.vjp(plain_scale, token_rows, norm_whole.astype(jnp.float32))
    mixer_input = lax.all_gather(first_norm.astype(jnp.bfloat16), "tensor", axis=0, tiled=True)
    query_proj = plain_product(mixer_input, query_whole)
    key_proj = plain_product(mixer_input, key_whole)
    value_proj = plain_product(mixer_input, value_whole)
    gate_proj = plain_product(mixer_input, gate_whole)
    beta_proj = plain_product(mixer_input, beta_whole)
    decay_proj = plain_product(mixer_input, decay_whole)
    total = mixer_input.shape[0]
    segment, valid, reset = group_layout(lengths[0], total, jnp.float32)

    def front_local(query_in, key_in, value_in, query_kernel, key_kernel, value_kernel):
        return mixer_front(
            query_in, key_in, value_in, query_kernel, key_kernel, value_kernel, segment
        )

    front_vals, front_pull = jax.vjp(
        front_local,
        query_proj,
        key_proj,
        value_proj,
        query_taps.astype(jnp.float32),
        key_taps.astype(jnp.float32),
        value_taps.astype(jnp.float32),
    )
    query_low = round_trip(front_vals[0])
    key_low = round_trip(front_vals[1])
    value_low = round_trip(front_vals[2])

    def rest_local(query_in, key_in, value_in, gate_in, beta_in, decay_in, rates, gains):
        return mixer_rest(
            query_in, key_in, value_in, gate_in, beta_in, decay_in, rates, gains, valid, reset
        )

    gated, rest_pull = jax.vjp(
        rest_local,
        query_low,
        key_low,
        value_low,
        gate_proj,
        beta_proj,
        decay_proj,
        decay_params,
        head_whole.astype(jnp.float32),
    )
    gated_rows = gated.astype(jnp.bfloat16)
    mixed = lax.psum_scatter(
        plain_product(gated_rows, out_whole), "tensor", scatter_dimension=0, tiled=True
    )
    middle = token_rows + mixed
    second_norm, second_pull = jax.vjp(plain_scale, middle, ffn_gain_whole.astype(jnp.float32))
    ffn_input = lax.all_gather(second_norm.astype(jnp.bfloat16), "tensor", axis=0, tiled=True)
    gate_act = plain_product(ffn_input, gate_ffn_whole)
    up_act = plain_product(ffn_input, up_ffn_whole)
    sigmoid_gate = jax.nn.sigmoid(gate_act)
    swish = gate_act * sigmoid_gate
    product_rows = (swish * up_act).astype(jnp.bfloat16)
    ffn_out = lax.psum_scatter(
        plain_product(product_rows, down_ffn_whole).astype(jnp.bfloat16),
        "tensor",
        scatter_dimension=0,
        tiled=True,
    ).astype(jnp.float32)
    block_out = (middle + ffn_out).astype(jnp.bfloat16)
    down_grad = lax.all_gather(cotangent, "tensor", axis=0, tiled=True)
    grad_ffn_down = transposed_product(product_rows, down_grad)
    grad_product = product_back(down_grad, down_ffn_whole)
    grad_gate_act = (
        grad_product * up_act * sigmoid_gate * (1.0 + gate_act * (1.0 - sigmoid_gate))
    ).astype(jnp.bfloat16)
    grad_up_act = (grad_product * swish).astype(jnp.bfloat16)
    grad_ffn_gate = transposed_product(ffn_input, grad_gate_act)
    grad_ffn_up = transposed_product(ffn_input, grad_up_act)
    ffn_input_part = product_back(grad_gate_act, gate_ffn_whole) + product_back(
        grad_up_act, up_ffn_whole
    )
    grad_second = lax.psum_scatter(ffn_input_part, "tensor", scatter_dimension=0, tiled=True)
    grad_middle_norm, grad_ffn_gain = second_pull(grad_second)
    grad_middle = cotangent.astype(jnp.float32) + grad_middle_norm
    grad_mixed = lax.all_gather(grad_middle.astype(jnp.bfloat16), "tensor", axis=0, tiled=True)
    grad_out_weight = transposed_product(gated_rows, grad_mixed)
    grad_gated = product_back(grad_mixed, out_whole)
    (
        grad_query_low,
        grad_key_low,
        grad_value_low,
        grad_gate_proj,
        grad_beta_proj,
        grad_decay_proj,
        grad_rates,
        grad_head_gain,
    ) = rest_pull(grad_gated)
    (
        grad_query_proj,
        grad_key_proj,
        grad_value_proj,
        grad_query_taps,
        grad_key_taps,
        grad_value_taps,
    ) = front_pull(
        (round_trip(grad_query_low), round_trip(grad_key_low), round_trip(grad_value_low))
    )
    rounded = [
        piece.astype(jnp.bfloat16)
        for piece in (
            grad_query_proj,
            grad_key_proj,
            grad_value_proj,
            grad_gate_proj,
            grad_beta_proj,
            grad_decay_proj,
        )
    ]
    weights_here = (query_whole, key_whole, value_whole, gate_whole, beta_whole, decay_whole)
    grad_query_weight = transposed_product(mixer_input, rounded[0])
    grad_key_weight = transposed_product(mixer_input, rounded[1])
    grad_value_weight = transposed_product(mixer_input, rounded[2])
    grad_gate_weight = transposed_product(mixer_input, rounded[3])
    grad_beta_weight = transposed_product(mixer_input, rounded[4])
    grad_decay_weight = transposed_product(mixer_input, rounded[5])
    mixer_input_part = product_back(rounded[0], weights_here[0])
    for index in range(1, 6):
        mixer_input_part = mixer_input_part + product_back(rounded[index], weights_here[index])
    grad_first = lax.psum_scatter(
        mixer_input_part.astype(jnp.bfloat16), "tensor", scatter_dimension=0, tiled=True
    ).astype(jnp.float32)
    grad_tokens_norm, grad_norm_gain = first_pull(grad_first)
    tokens_grad = grad_middle + grad_tokens_norm
    heads_here = decay_params.shape[1]
    rate_spread = lax.dynamic_update_slice(
        jnp.zeros((2, H), jnp.float32), grad_rates, (0, lax.axis_index("tensor") * heads_here)
    )
    norm_total, ffn_total, rate_total = lax.psum(
        (grad_norm_gain, grad_ffn_gain, rate_spread), ("dp", "tensor")
    )
    share = norm_gain.shape[0]
    begin = lax.axis_index("dp") * share
    norm_gain_grad = lax.dynamic_slice_in_dim(norm_total, begin, share)
    ffn_gain_grad = lax.dynamic_slice_in_dim(ffn_total, begin, share)
    decay_params_grad = lax.dynamic_slice_in_dim(
        rate_total, lax.axis_index("tensor") * heads_here, heads_here, axis=1
    )
    summed = (
        lax.psum_scatter(grad_query_weight, "dp", scatter_dimension=0, tiled=True),
        lax.psum_scatter(grad_key_weight, "dp", scatter_dimension=0, tiled=True),
        lax.psum_scatter(grad_value_weight, "dp", scatter_dimension=0, tiled=True),
        lax.psum_scatter(grad_gate_weight, "dp", scatter_dimension=0, tiled=True),
        lax.psum_scatter(grad_beta_weight, "dp", scatter_dimension=0, tiled=True),
        lax.psum_scatter(grad_decay_weight, "dp", scatter_dimension=0, tiled=True),
        lax.psum_scatter(grad_query_taps, "dp", scatter_dimension=1, tiled=True),
        lax.psum_scatter(grad_key_taps, "dp", scatter_dimension=1, tiled=True),
        lax.psum_scatter(grad_value_taps, "dp", scatter_dimension=1, tiled=True),
        lax.psum_scatter(grad_head_gain, "dp", scatter_dimension=0, tiled=True),
        lax.psum_scatter(grad_out_weight, "dp", scatter_dimension=1, tiled=True),
        lax.psum_scatter(grad_ffn_gate, "dp", scatter_dimension=0, tiled=True),
        lax.psum_scatter(grad_ffn_up, "dp", scatter_dimension=0, tiled=True),
        lax.psum_scatter(grad_ffn_down, "dp", scatter_dimension=1, tiled=True),
    )
    return (
        block_out,
        tokens_grad,
        norm_gain_grad,
        summed[0],
        summed[1],
        summed[2],
        summed[3],
        summed[4],
        summed[5],
        summed[6],
        summed[7],
        summed[8],
        decay_params_grad,
        summed[9],
        summed[10],
        ffn_gain_grad,
        summed[11],
        summed[12],
        summed[13],
    )


def solution(mesh):
    return jax.shard_map(
        local,
        mesh=mesh,
        in_specs=(
            P(("dp", "tensor"), None),
            P("dp", None),
            P(("dp", "tensor"), None),
            P("dp"),
            P("dp", "tensor"),
            P("dp", "tensor"),
            P("dp", "tensor"),
            P("dp", "tensor"),
            P("dp", "tensor"),
            P("dp", "tensor"),
            P(None, ("tensor", "dp")),
            P(None, ("tensor", "dp")),
            P(None, ("tensor", "dp")),
            P(None, "tensor"),
            P(("tensor", "dp")),
            P("tensor", "dp"),
            P("dp"),
            P("dp", "tensor"),
            P("dp", "tensor"),
            P("tensor", "dp"),
        ),
        out_specs=(
            P(("dp", "tensor"), None),
            P(("dp", "tensor"), None),
            P("dp"),
            P("dp", "tensor"),
            P("dp", "tensor"),
            P("dp", "tensor"),
            P("dp", "tensor"),
            P("dp", "tensor"),
            P("dp", "tensor"),
            P(None, ("tensor", "dp")),
            P(None, ("tensor", "dp")),
            P(None, ("tensor", "dp")),
            P(None, "tensor"),
            P(("tensor", "dp")),
            P("tensor", "dp"),
            P("dp"),
            P("dp", "tensor"),
            P("dp", "tensor"),
            P("tensor", "dp"),
        ),
        check_vma=False,
    )
```

profile of v0, /device:TPU:0, one launch (start us, length us, event | category | flops | bytes accessed | tf_op | source)
XLA Modules:
  0.0 2069.4 jit_solution(18406226151296467483)
XLA Ops:
  9.0 22.3 %all-gather = bf16[8,1,128]{2,1,0:T(2,128)(2,1)S(1)} all-gather(bf16[1,1,128]{2,1,0:T(2,128)(2,1)} %bitcast.1079), channel_id=1, replica_groups=mesh['dp'=8,'tensor'=4] {'dp'}, dimensions={0}, use_global_device_ids=true | all-gather | bytes 2304 | tf_op jit(solution)/shard_map/all_gather | solution.py:187
  40.4 31.7 %all_gather.68 = bf16[1024,256]{1,0:T(8,128)(2,1)S(1)} all-gather(bf16[128,256]{1,0:T(8,128)(2,1)S(1)} %copy-done.57), channel_id=1, replica_groups=mesh['dp'=8,'tensor'=4] {'dp'}, dimensions={0}, use_global_device_ids=true | all-gather | bytes 589824 | tf_op jit(solution)/shard_map/all_gather | solution.py:188
  72.1 32.0 %all_gather.63 = bf16[1024,256]{1,0:T(8,128)(2,1)S(1)} all-gather(bf16[128,256]{1,0:T(8,128)(2,1)S(1)} %copy-done.58), channel_id=1, replica_groups=mesh['dp'=8,'tensor'=4] {'dp'}, dimensions={0}, use_global_device_ids=true | all-gather | bytes 589824 | tf_op jit(solution)/shard_map/all_gather | solution.py:189
  104.0 16.4 all-gather.1
  120.6 18.3 all-gather.3
  139.0 16.5 all-gather.2
  155.6 18.1 all_gather.62
  175.0 16.3 all_gather.65
  192.8 19.0 all-reduce.37
  226.8 212.5 %while.91 = (s32[]{:T(128)}, f32[1,256,512]{2,1,0:T(8,128)S(1)}, f32[8,64,1,512]{3,1,2,0:T(8,128)}, f32[8]{0:T(128)}, f32[8,1,64,64]{3,2,1,0:T(8,128)}, /*index=...) while((s32[]{:T(128)}, f32[1,256,512]{2,1,0:T(8,128)S(1)}, ...), condition=%wide.region_5.6_spmd.clone.clone.clone, body=%wide.region_3.5_spmd.clone.clone.sunk.clone | while | flops 391729408 | bytes 7396758 | solution.py:126
  231.6 4.9 custom-call.49
  258.2 4.9 custom-call.49
  284.8 4.9 custom-call.49
  311.2 4.9 custom-call.49
  337.8 4.9 custom-call.49
  364.4 4.9 custom-call.49
  391.0 4.9 custom-call.49
  417.5 4.9 custom-call.49
  440.9 3.4 multiply_convert_fusion.3
  444.3 3.5 fusion.250
  448.4 16.5 all-gather.4
  465.0 11.4 reduce-scatter.28.cloned.1.call-done
  480.6 41.7 %all-gather.26.cloned.1.call-done = bf16[1024,704]{0,1:T(8,128)(2,1)} async-done(((bf16[128,704]{0,1:T(8,128)(2,1)}), bf16[1024,704]{0,1:T(8,128)(2,1)}) %all-gather.26.cloned.1.call-update) | async-done | bytes 1441808 | tf_op jit(solution)/shard_map/all_gather | solution.py:200
  522.4 17.4 all-gather.24.cloned.1.call-done
  539.7 3.8 fusion.251
  543.5 42.3 %all-gather.28.cloned.1.call-done = bf16[1024,704]{0,1:T(8,128)(2,1)} async-done(((bf16[128,704]{0,1:T(8,128)(2,1)}), bf16[1024,704]{0,1:T(8,128)(2,1)}) %all-gather.28.cloned.1.call-update) | async-done | bytes 1441808 | tf_op jit(solution)/shard_map/all_gather | solution.py:201
  585.8 3.7 fusion.252
  589.5 13.1 all-gather.32.cloned.1.call-done
  602.6 45.9 %all-gather.30.cloned.1.call-done = bf16[704,1024]{1,0:T(8,128)(2,1)} async-done(((bf16[704,128]{1,0:T(8,128)(2,1)}), bf16[704,1024]{1,0:T(8,128)(2,1)}) %all-gather.30.cloned.1.call-update) | async-done | bytes 1441808 | tf_op jit(solution)/shard_map/all_gather | solution.py:202
  648.5 5.0 multiply_convert_fusion
  657.9 29.9 %reduce-scatter.32.cloned.1.call-done = f32[128,1024]{1,0:T(8,128)} async-done(((f32[512,1024]{1,0:T(8,128)}), f32[128,1024]{1,0:T(8,128)}) %reduce-scatter.32.cloned.1.call-update) | async-done | bytes 524304 | tf_op jit(solution)/shard_map/reduce_scatter | solution.py:281
  700.1 8.3 all-gather.34.cloned.1.call-done
  708.5 5.0 multiply_reduce_fusion
  716.3 385.8 %while.92 = (s32[]{:T(128)}, f32[1,256,512]{1,2,0:T(8,128)S(1)}, bf16[8,64,1,256]{3,1,2,0:T(8,128)(2,1)}, bf16[8,64,1,256]{3,1,2,0:T(8,128)(2,1)}, bf16[8,64,1,5...) while((s32[]{:T(128)}, f32[1,256,512]{1,2,0:T(8,128)S(1)}, ...), condition=%wide.region_24.25_spmd.clone.clone.clone, body=%wide.region_13.24_spmd.clone.clone.sunk.clone | while | flops 785240576 | bytes 14192249 | solution.py:126
  723.1 4.9 custom-call.50
  771.2 4.9 custom-call.50
  819.4 4.9 custom-call.50
  867.7 4.9 custom-call.50
  915.9 4.9 custom-call.50
  964.2 4.9 custom-call.50
  1012.4 4.9 custom-call.50
  1060.6 4.9 custom-call.50
  1104.1 2.8 multiply_reduce_fusion.15
  1117.0 9.1 reduce-scatter.56.cloned.1.call-start
  1140.4 2.5 add_convert_fusion.1
  1147.2 3.4 convolution_convert_fusion
  1150.7 3.6 fusion.263
  1154.4 3.6 fusion.264
  1159.2 2.5 fusion.262
  1174.7 21.3 %all-reduce.38 = f32[512]{0:T(512)S(1)} all-reduce(f32[512]{0:T(512)S(1)} %copy-done.114), channel_id=15, replica_groups=mesh['dp'=8,'tensor'=4] {'dp'}, use_global_device_ids=true, to_apply=%region_56.57.clone | all-reduce | flops 512 | bytes 4096
  1198.7 42.4 %reduce-scatter.56.cloned.1.call-done = f32[32,4]{1,0:T(8,128)} async-done(((f32[256,4]{1,0:T(8,128)}), f32[32,4]{1,0:T(8,128)}) %reduce-scatter.56.cloned.1.call-update) | async-done | bytes 528
  1242.5 63.4 %reduce-scatter.52.cloned.1.call-done = f32[128,1]{1,0:T(8,128)} async-done(((f32[1024,1]{1,0:T(8,128)}), f32[128,1]{1,0:T(8,128)}) %reduce-scatter.52.cloned.1.call-update) | async-done | bytes 528
  1307.4 63.0 %reduce-scatter.54.cloned.1.call-done = f32[128,1]{1,0:T(8,128)} async-done(((f32[1024,1]{1,0:T(8,128)}), f32[128,1]{1,0:T(8,128)}) %reduce-scatter.54.cloned.1.call-update) | async-done | bytes 528
  1371.8 62.6 %reduce-scatter.60.cloned.1.call-done = f32[64,4]{1,0:T(8,128)} async-done(((f32[512,4]{1,0:T(8,128)}), f32[64,4]{1,0:T(8,128)}) %reduce-scatter.60.cloned.1.call-update) | async-done | bytes 1040
  1435.8 25.0 %reduce-scatter.34.cloned.1.call-done = bf16[128,1024]{1,0:T(8,128)(2,1)} async-done(((bf16[512,1024]{1,0:T(8,128)(2,1)}), bf16[128,1024]{1,0:T(8,128)(2,1)}) %reduce-scatter.34.cloned.1.call-update) | async-done | bytes 262160 | tf_op jit(solution)/shard_map/reduce_scatter | solution.py:328
  1462.0 39.5 %all-reduce.39 = (f32[1024]{0:T(1024)S(1)}, f32[2,4]{0,1:T(4,128)S(1)}, f32[1024]{0:T(1024)S(1)}) all-reduce(f32[1024]{0:T(1024)S(1)} %get-tuple-element.1946, f32[2,4]{0,1:T(4,128)S(1)} %dynamic_update_slice.208, f32[1024]{0:T(1024)S(1)} %copy-done.81), channel_id=1, replica_groups=mesh['dp'=8,'tensor'=4] {'dp','tensor'}, use_global_device_ids=true, to_apply=%region_30.31 | all-reduce | flops 2056 | bytes 16448 | tf_op jit(solution)/shard_map/psum | solution.py:337
  1505.5 59.2 %reduce-scatter.46.cloned.1.call-done = f32[128,704]{0,1:T(8,128)} async-done(((f32[1024,704]{0,1:T(8,128)}), f32[128,704]{0,1:T(8,128)}) %reduce-scatter.46.cloned.1.call-update) | async-done | bytes 360464 | tf_op jit(solution)/shard_map/reduce_scatter | solution.py:359
  1564.7 75.7 %reduce-scatter.48.cloned.1.call-done = f32[128,704]{0,1:T(8,128)} async-done(((f32[1024,704]{0,1:T(8,128)}), f32[128,704]{0,1:T(8,128)}) %reduce-scatter.48.cloned.1.call-update) | async-done | bytes 360464 | tf_op jit(solution)/shard_map/reduce_scatter | solution.py:360
  1640.4 75.7 %reduce-scatter.50.cloned.1.call-done = f32[704,128]{1,0:T(8,128)} async-done(((f32[704,1024]{1,0:T(8,128)}), f32[704,128]{1,0:T(8,128)}) %reduce-scatter.50.cloned.1.call-update) | async-done | bytes 360464 | tf_op jit(solution)/shard_map/reduce_scatter | solution.py:361
  1716.1 66.7 %reduce-scatter.38.cloned.1.call-done = f32[128,256]{1,0:T(8,128)} async-done(((f32[1024,256]{1,0:T(8,128)}), f32[128,256]{1,0:T(8,128)}) %reduce-scatter.38.cloned.1.call-update) | async-done | bytes 131088 | tf_op jit(solution)/shard_map/reduce_scatter | solution.py:349
  1782.8 66.7 %reduce-scatter.36.cloned.1.call-done = f32[128,256]{1,0:T(8,128)} async-done(((f32[1024,256]{1,0:T(8,128)}), f32[128,256]{1,0:T(8,128)}) %reduce-scatter.36.cloned.1.call-update) | async-done | bytes 131088 | tf_op jit(solution)/shard_map/reduce_scatter | solution.py:348
  1849.6 71.3 %reduce-scatter.44.cloned.1.call-done = f32[512,128]{1,0:T(8,128)} async-done(((f32[512,1024]{1,0:T(8,128)}), f32[512,128]{1,0:T(8,128)}) %reduce-scatter.44.cloned.1.call-update) | async-done | bytes 262160 | tf_op jit(solution)/shard_map/reduce_scatter | solution.py:358
  1920.8 70.9 %reduce-scatter.40.cloned.1.call-done = f32[128,512]{1,0:T(8,128)} async-done(((f32[1024,512]{1,0:T(8,128)}), f32[128,512]{1,0:T(8,128)}) %reduce-scatter.40.cloned.1.call-update) | async-done | bytes 262160 | tf_op jit(solution)/shard_map/reduce_scatter | solution.py:350
  1991.7 70.6 %reduce-scatter.42.cloned.1.call-done = f32[128,512]{1,0:T(8,128)} async-done(((f32[1024,512]{1,0:T(8,128)}), f32[128,512]{1,0:T(8,128)}) %reduce-scatter.42.cloned.1.call-update) | async-done | bytes 262160 | tf_op jit(solution)/shard_map/reduce_scatter | solution.py:351
  (1098 shorter events, 604.9 us)
Async XLA Ops:
  7.2 184.1 %copy-start.113 = (u32[32]{0:T(128)S(1)}, u32[32]{0:T(128)}, u32[]{:S(2)}) copy-start(u32[32]{0:T(128)} %constant.376) | copy-start | bytes 388
  7.2 96.8 %copy-start.119 = (bf16[4,32]{1,0:T(4,128)(2,1)S(1)}, bf16[4,32]{1,0:T(4,128)(2,1)}, u32[]{:S(2)}) copy-start(bf16[4,32]{1,0:T(4,128)(2,1)} %param.35) | copy-start | bytes 772
  7.2 113.3 %copy-start.120 = (bf16[4,32]{1,0:T(4,128)(2,1)S(1)}, bf16[4,32]{1,0:T(4,128)(2,1)}, u32[]{:S(2)}) copy-start(bf16[4,32]{1,0:T(4,128)(2,1)} %param.34) | copy-start | bytes 772
  7.2 131.7 %copy-start.121 = (bf16[4,64]{1,0:T(4,128)(2,1)S(1)}, bf16[4,64]{1,0:T(4,128)(2,1)}, u32[]{:S(2)}) copy-start(bf16[4,64]{1,0:T(4,128)(2,1)} %param.36) | copy-start | bytes 1540
  7.3 148.3 %copy-start.124 = (bf16[128,1]{0,1:T(2,128)(2,1)S(1)}, bf16[128,1]{0,1:T(2,128)(2,1)}, u32[]{:S(2)}) copy-start(bf16[128,1]{0,1:T(2,128)(2,1)} %param.33) | copy-start | bytes 772
  7.3 166.5 %copy-start.115 = (f32[2,1]{0,1:T(1,128)S(1)}, f32[2,1]{0,1:T(1,128)}, u32[]{:S(2)}) copy-start(f32[2,1]{0,1:T(1,128)} %param.37) | copy-start | bytes 28
  7.3 167.7 %copy-start.125 = (bf16[128,1]{0,1:T(2,128)(2,1)S(1)}, bf16[128,1]{0,1:T(2,128)(2,1)}, u32[]{:S(2)}) copy-start(bf16[128,1]{0,1:T(2,128)(2,1)} %param.32) | copy-start | bytes 772
  7.3 185.3 %copy-start.129 = (bf16[64]{0:T(256)(128)(2,1)S(1)}, bf16[64]{0:T(256)(128)(2,1)}, u32[]{:S(2)}) copy-start(bf16[64]{0:T(256)(128)(2,1)} %param.38) | copy-start | bytes 388
  7.3 204.6 %all-gather.16.cloned.1.call-start = ((), (), s32[]{:S(2)}) async-start(), calls=%async_computation.17 | async-start | bytes 1310720 | tf_op jit(solution)/shard_map/all_gather | solution.py:206
  9.0 204.7 %copy-start.109 = (f32[128]{0:T(128)}, f32[128]{0:T(128)S(1)}, u32[]{:S(2)}) copy-start(f32[128]{0:T(128)S(1)} %fusion.225) | copy-start | bytes 1540
  33.1 186.5 %all-gather.18.cloned.1.call-start = ((), (), s32[]{:S(2)}) async-start(), calls=%async_computation.18 | async-start | bytes 1179648 | tf_op jit(solution)/shard_map/all_gather | solution.py:190
  33.8 407.1 %all-gather.20.cloned.1.call-start = ((), (), s32[]{:S(2)}) async-start(), calls=%async_computation.19 | async-start | bytes 1179648 | tf_op jit(solution)/shard_map/all_gather | solution.py:191
  34.6 409.7 %all-gather.22.cloned.1.call-start = ((), (), s32[]{:S(2)}) async-start(), calls=%async_computation.20 | async-start | bytes 1179648 | tf_op jit(solution)/shard_map/all_gather | solution.py:198
  35.1 441.3 %reduce-scatter.28.cloned.1.call-start = ((), (), s32[]{:S(2)}) async-start(), calls=%async_computation.21 | async-start | bytes 2621440 | tf_op jit(solution)/shard_map/reduce_scatter | solution.py:251
  40.3 181.3 %copy-start.103 = (pred[512]{0:T(512)(128)(4,1)}, pred[512]{0:T(512)(128)(4,1)S(1)}, u32[]{:S(2)}) copy-start(pred[512]{0:T(512)(128)(4,1)S(1)} %concatenate.50) | copy-start | bytes 1540
  40.4 181.2 %copy-start.105 = (pred[512]{0:T(512)(128)(4,1)}, pred[512]{0:T(512)(128)(4,1)S(1)}, u32[]{:S(2)}) copy-start(pred[512]{0:T(512)(128)(4,1)S(1)} %concatenate.52) | copy-start | bytes 1540
  72.1 142.1 %copy-start.24 = (bf16[1024,256]{1,0:T(8,128)(2,1)}, bf16[1024,256]{1,0:T(8,128)(2,1)S(1)}, u32[]{:S(2)}) copy-start(bf16[1024,256]{1,0:T(8,128)(2,1)S(1)} %all_gather.68) | copy-start | bytes 1572868
  104.0 110.1 %copy-start.26 = (bf16[1024,256]{1,0:T(8,128)(2,1)}, bf16[1024,256]{1,0:T(8,128)(2,1)S(1)}, u32[]{:S(2)}) copy-start(bf16[1024,256]{1,0:T(8,128)(2,1)S(1)} %all_gather.63) | copy-start | bytes 1572868
  120.5 93.6 %copy-start.85 = (f32[1,256]{1,0:T(1,128)}, f32[1,256]{1,0:T(1,128)S(1)}, u32[]{:S(2)}) copy-start(f32[1,256]{1,0:T(1,128)S(1)} %get-tuple-element.2169) | copy-start | bytes 3076
  120.5 93.7 %copy-start.89 = (f32[1,256]{1,0:T(1,128)}, f32[1,256]{1,0:T(1,128)S(1)}, u32[]{:S(2)}) copy-start(f32[1,256]{1,0:T(1,128)S(1)} %get-tuple-element.2172) | copy-start | bytes 3076
  120.5 93.7 %copy-start.93 = (f32[1,256]{1,0:T(1,128)}, f32[1,256]{1,0:T(1,128)S(1)}, u32[]{:S(2)}) copy-start(f32[1,256]{1,0:T(1,128)S(1)} %get-tuple-element.2171) | copy-start | bytes 3076
  120.5 93.7 %copy-start.95 = (f32[1,256]{1,0:T(1,128)}, f32[1,256]{1,0:T(1,128)S(1)}, u32[]{:S(2)}) copy-start(f32[1,256]{1,0:T(1,128)S(1)} %get-tuple-element.2170) | copy-start | bytes 3076
  138.9 75.3 %copy-start.87 = (f32[1,256]{1,0:T(1,128)}, f32[1,256]{1,0:T(1,128)S(1)}, u32[]{:S(2)}) copy-start(f32[1,256]{1,0:T(1,128)S(1)} %get-tuple-element.2165) | copy-start | bytes 3076
  138.9 75.3 %copy-start.91 = (f32[1,256]{1,0:T(1,128)}, f32[1,256]{1,0:T(1,128)S(1)}, u32[]{:S(2)}) copy-start(f32[1,256]{1,0:T(1,128)S(1)} %get-tuple-element.2168) | copy-start | bytes 3076
  138.9 75.3 %copy-start.97 = (f32[1,256]{1,0:T(1,128)}, f32[1,256]{1,0:T(1,128)S(1)}, u32[]{:S(2)}) copy-start(f32[1,256]{1,0:T(1,128)S(1)} %get-tuple-element.2167) | copy-start | bytes 3076
  138.9 75.3 %copy-start.99 = (f32[1,256]{1,0:T(1,128)}, f32[1,256]{1,0:T(1,128)S(1)}, u32[]{:S(2)}) copy-start(f32[1,256]{1,0:T(1,128)S(1)} %get-tuple-element.2166) | copy-start | bytes 3076
  155.5 66.1 %copy-start.63 = (f32[1,512]{1,0:T(1,128)}, f32[1,512]{1,0:T(1,128)S(1)}, u32[]{:S(2)}) copy-start(f32[1,512]{1,0:T(1,128)S(1)} %get-tuple-element.2160) | copy-start | bytes 6148
  155.5 66.1 %copy-start.65 = (f32[1,512]{1,0:T(1,128)}, f32[1,512]{1,0:T(1,128)S(1)}, u32[]{:S(2)}) copy-start(f32[1,512]{1,0:T(1,128)S(1)} %get-tuple-element.2163) | copy-start | bytes 6148
  155.5 66.1 %copy-start.67 = (f32[1,512]{1,0:T(1,128)}, f32[1,512]{1,0:T(1,128)S(1)}, u32[]{:S(2)}) copy-start(f32[1,512]{1,0:T(1,128)S(1)} %get-tuple-element.2161) | copy-start | bytes 6148
  155.6 66.1 %copy-start.69 = (f32[1,512]{1,0:T(1,128)}, f32[1,512]{1,0:T(1,128)S(1)}, u32[]{:S(2)}) copy-start(f32[1,512]{1,0:T(1,128)S(1)} %get-tuple-element.2162) | copy-start | bytes 6148
  211.9 479.7 %copy-start.107 = (pred[512]{0:T(512)(128)(4,1)}, pred[512]{0:T(512)(128)(4,1)S(1)}, u32[]{:S(2)}) copy-start(pred[512]{0:T(512)(128)(4,1)S(1)} %pad_add_fusion.6) | copy-start | bytes 1540
  447.8 74.6 %all-gather.26.cloned.1.call-start = ((), (), s32[]{:S(2)}) async-start(), calls=%async_computation.23 | async-start | bytes 1622016 | tf_op jit(solution)/shard_map/all_gather | solution.py:200
  448.4 91.3 %all-gather.24.cloned.1.call-start = ((), (), s32[]{:S(2)}) async-start(), calls=%async_computation.22 | async-start | bytes 1310720 | tf_op jit(solution)/shard_map/all_gather | solution.py:256
  477.6 212.0 %copy-start.6 = (f32[128,1024]{1,0:T(8,128)}, f32[128,1024]{1,0:T(8,128)S(1)}, u32[]{:S(2)}) copy-start(f32[128,1024]{1,0:T(8,128)S(1)} %get-tuple-element.2105) | copy-start | bytes 1572868
  477.6 212.0 %copy-start.101 = (f32[128]{0:T(128)}, f32[128]{0:T(128)S(1)}, u32[]{:S(2)}) copy-start(f32[128]{0:T(128)S(1)} %fusion.226) | copy-start | bytes 1540
  478.5 107.3 %all-gather.28.cloned.1.call-start = ((), (), s32[]{:S(2)}) async-start(), calls=%async_computation.24 | async-start | bytes 1622016 | tf_op jit(solution)/shard_map/all_gather | solution.py:201
  479.3 123.3 %all-gather.32.cloned.1.call-start = ((), (), s32[]{:S(2)}) async-start(), calls=%async_computation.27 | async-start | bytes 1310720 | tf_op jit(solution)/shard_map/all_gather | solution.py:269
  480.0 168.6 %all-gather.30.cloned.1.call-start = ((), (), s32[]{:S(2)}) async-start(), calls=%async_computation.25 | async-start | bytes 1622016 | tf_op jit(solution)/shard_map/all_gather | solution.py:202
  480.6 207.2 %reduce-scatter.32.cloned.1.call-start = ((), (), s32[]{:S(2)}) async-start(), calls=%async_computation.28 | async-start | bytes 2621440 | tf_op jit(solution)/shard_map/reduce_scatter | solution.py:281
  657.8 50.6 %all-gather.34.cloned.1.call-start = ((), (), s32[]{:S(2)}) async-start(), calls=%async_computation.29 | async-start | bytes 1310720 | tf_op jit(solution)/shard_map/all_gather | solution.py:284
  691.6 505.8 %reduce-scatter.58.cloned.1.call-start = ((), (), s32[]{:S(2)}) async-start(), calls=%async_computation.42 | async-start | bytes 147456
  1117.0 124.1 %reduce-scatter.56.cloned.1.call-start = ((), (), s32[]{:S(2)}) async-start(), calls=%async_computation.41 | async-start | bytes 147456
  1136.7 169.3 %reduce-scatter.52.cloned.1.call-start = ((), (), s32[]{:S(2)}) async-start(), calls=%async_computation.39 | async-start | bytes 589824
  1138.0 232.3 %reduce-scatter.54.cloned.1.call-start = ((), (), s32[]{:S(2)}) async-start(), calls=%async_computation.40 | async-start | bytes 589824
  1139.4 295.0 %reduce-scatter.60.cloned.1.call-start = ((), (), s32[]{:S(2)}) async-start(), calls=%async_computation.43 | async-start | bytes 294912
  1140.4 320.5 %reduce-scatter.34.cloned.1.call-start = ((), (), s32[]{:S(2)}) async-start(), calls=%async_computation.30 | async-start | bytes 1310720 | tf_op jit(solution)/shard_map/reduce_scatter | solution.py:328
  1147.2 356.1 %reduce-scatter.30.cloned.1.call-start = ((), (), s32[]{:S(2)}) async-start(), calls=%async_computation.26 | async-start | bytes 1310720 | tf_op jit(solution)/shard_map/reduce_scatter | solution.py:262
  1150.7 414.0 %reduce-scatter.46.cloned.1.call-start = ((), (), s32[]{:S(2)}) async-start(), calls=%async_computation.36 | async-start | bytes 3244032 | tf_op jit(solution)/shard_map/reduce_scatter | solution.py:359
  1154.3 486.1 %reduce-scatter.48.cloned.1.call-start = ((), (), s32[]{:S(2)}) async-start(), calls=%async_computation.37 | async-start | bytes 3244032 | tf_op jit(solution)/shard_map/reduce_scatter | solution.py:360
  1158.0 558.1 %reduce-scatter.50.cloned.1.call-start = ((), (), s32[]{:S(2)}) async-start(), calls=%async_computation.38 | async-start | bytes 3244032 | tf_op jit(solution)/shard_map/reduce_scatter | solution.py:361
  1161.8 621.0 %reduce-scatter.38.cloned.1.call-start = ((), (), s32[]{:S(2)}) async-start(), calls=%async_computation.32 | async-start | bytes 1179648 | tf_op jit(solution)/shard_map/reduce_scatter | solution.py:349
  1164.3 685.3 %reduce-scatter.36.cloned.1.call-start = ((), (), s32[]{:S(2)}) async-start(), calls=%async_computation.31 | async-start | bytes 1179648 | tf_op jit(solution)/shard_map/reduce_scatter | solution.py:348
  1165.8 755.0 %reduce-scatter.44.cloned.1.call-start = ((), (), s32[]{:S(2)}) async-start(), calls=%async_computation.35 | async-start | bytes 2359296 | tf_op jit(solution)/shard_map/reduce_scatter | solution.py:358
  1168.1 823.7 %reduce-scatter.40.cloned.1.call-start = ((), (), s32[]{:S(2)}) async-start(), calls=%async_computation.33 | async-start | bytes 2359296 | tf_op jit(solution)/shard_map/reduce_scatter | solution.py:350
  1170.2 892.1 %reduce-scatter.42.cloned.1.call-start = ((), (), s32[]{:S(2)}) async-start(), calls=%async_computation.34 | async-start | bytes 2359296 | tf_op jit(solution)/shard_map/reduce_scatter | solution.py:351
  1173.2 287.6 %copy-start.19 = (bf16[128,1024]{1,0:T(8,128)(2,1)S(1)}, bf16[128,1024]{1,0:T(8,128)(2,1)}, u32[]{:S(2)}) copy-start(bf16[128,1024]{1,0:T(8,128)(2,1)} %param.24) | copy-start | bytes 786436
  1173.2 287.6 %copy-start.110 = (f32[128]{0:T(128)S(1)}, f32[128]{0:T(128)}, u32[]{:S(2)}) copy-start(f32[128]{0:T(128)} %copy-done.109) | copy-start | bytes 1540
  1173.2 288.8 %copy-start.81 = (f32[1024]{0:T(1024)S(1)}, f32[1024]{0:T(1024)}, u32[]{:S(2)}) copy-start(f32[1024]{0:T(1024)} %get-tuple-element.1932) | copy-start | bytes 12292
  1173.2 330.0 %copy-start.123 = (f32[128]{0:T(128)S(1)}, f32[128]{0:T(128)}, u32[]{:S(2)}) copy-start(f32[128]{0:T(128)} %copy-done.122) | copy-start | bytes 1540
  1173.3 330.0 %copy-start.7 = (f32[128,1024]{1,0:T(8,128)S(1)}, f32[128,1024]{1,0:T(8,128)}, u32[]{:S(2)}) copy-start(f32[128,1024]{1,0:T(8,128)} %copy-done.6) | copy-start | bytes 1572868
  1173.3 330.0 %copy-start.23 = (f32[128,1024]{1,0:T(8,128)S(1)}, f32[128,1024]{1,0:T(8,128)}, u32[]{:S(2)}) copy-start(f32[128,1024]{1,0:T(8,128)} %reduce-scatter.32.cloned.1.call-done) | copy-start | bytes 1572868
  1173.3 330.0 %copy-start.38 = (bf16[128,1024]{1,0:T(8,128)(2,1)S(1)}, bf16[128,1024]{1,0:T(8,128)(2,1)}, u32[]{:S(2)}) copy-start(bf16[128,1024]{1,0:T(8,128)(2,1)} %param.26) | copy-start | bytes 786436
  1173.3 330.0 %copy-start.102 = (f32[128]{0:T(128)S(1)}, f32[128]{0:T(128)}, u32[]{:S(2)}) copy-start(f32[128]{0:T(128)} %copy-done.101) | copy-start | bytes 1540
  1173.3 330.0 %copy-start.112 = (f32[128]{0:T(128)S(1)}, f32[128]{0:T(128)}, u32[]{:S(2)}) copy-start(f32[128]{0:T(128)} %copy-done.111) | copy-start | bytes 1540
  (128 other events, 758.2 us)
Sparse Core Ops, SparseCore 0:
  33.2 14.0 all-gather.15
  49.4 42.6 all-gather.17
  94.2 40.5 all-gather.19
  136.8 38.4 all-gather.21
  447.9 28.4 reduce-scatter.27
  478.5 43.8 all-gather.25
  524.6 15.1 all-gather.23
  542.0 43.8 all-gather.27
  587.5 15.1 all-gather.31
  604.7 43.8 all-gather.29
  658.0 29.7 reduce-scatter.31
  691.7 16.7 all-gather.33
  1117.2 60.8 reduce-scatter.57
  1181.2 59.8 reduce-scatter.55
  1244.9 60.9 reduce-scatter.51
  1309.5 60.8 reduce-scatter.53
  1374.1 60.2 reduce-scatter.59
  1436.8 23.9 reduce-scatter.33
  1463.5 24.8 reduce-scatter.29
  1492.4 72.2 reduce-scatter.45
  1568.8 71.5 reduce-scatter.47
  1644.5 71.5 reduce-scatter.49
  1720.1 62.6 reduce-scatter.37
  1787.0 62.4 reduce-scatter.35
  1853.7 67.1 reduce-scatter.43
  1924.8 66.8 reduce-scatter.39
  1995.7 66.6 reduce-scatter.41
where the time goes:
time: 2090 us; the launch traced here: 2070 us
  waiting for transfers between devices  1030 us (49%)
  matrix products  292 us (14%)
  blocking collectives  268 us (13%)
  other arithmetic  253 us (12%)
  local copies, waits for them, and re-layouts  175 us (8%)
  loops' own time  23.4 us (1%)
    unnamed x32, waiting for transfers between devices  236 us
    dynamic_slice x88, local copies, waits for them, and re-layouts, mixer_rest(): lax.scan(block_step, start_state, (into_blocks(query), into_blocks(key),...  88.6 us
    another operation x48, other arithmetic, block_step(): lax.linalg.triangular_solve(system, right_heads, left_side=True, lower=Tr...  85.9 us
    reduce_scatter x1, waiting for transfers between devices, local(): lax.psum_scatter(grad_ffn_up, 'dp', scatter_dimension=0, tiled=True)  75.7 us
    reduce_scatter x1, waiting for transfers between devices, local(): lax.psum_scatter(grad_ffn_down, 'dp', scatter_dimension=1, tiled=True)  75.7 us
    reduce_scatter x1, waiting for transfers between devices, local(): lax.psum_scatter(grad_out_weight, 'dp', scatter_dimension=1, tiled=True)  71.3 us
    reduce_scatter x1, waiting for transfers between devices, local(): lax.psum_scatter(grad_value_weight, 'dp', scatter_dimension=0, tiled=True)  70.9 us
    reduce_scatter x1, waiting for transfers between devices, local(): lax.psum_scatter(grad_gate_weight, 'dp', scatter_dimension=0, tiled=True)  70.6 us
  transfers between devices with their start and end apart: 27, of which 21 were waited for; matrix products, arithmetic and copies ran while one was open for 15% of the time, Pallas kernels for 0%

commit v1 on v0

v1 whole, which is shorter than its diff:
```python
import jax
import jax.numpy as jnp
from jax import lax
from jax.experimental import pallas as pl
from jax.experimental.pallas import tpu as pltpu
from jax.sharding import PartitionSpec as P

DK = 256
DV = 512
BLOCK = 64
SPAN = 256
PART = 128
TOTAL = 512
FRONT = 2 * DK + DV
WIDE = FRONT + 128
BLOCKS = TOTAL // BLOCK
SPANS = TOTAL // SPAN
F32 = jnp.float32
BF16 = jnp.bfloat16
SMEM = pltpu.SMEM
VMEM = pltpu.VMEM
LIMIT = 56 * 1024 * 1024


def mul(left, right):
    return lax.dot_general(left, right, (((1,), (0,)), ((), ())), preferred_element_type=F32)


def mul_nt(left, right):
    return lax.dot_general(left, right, (((1,), (1,)), ((), ())), preferred_element_type=F32)


def mul_tn(left, right):
    return lax.dot_general(left, right, (((0,), (0,)), ((), ())), preferred_element_type=F32)


def low(value):
    return value.astype(BF16)


def halves(value):
    high = low(value)
    return high, low(value - high.astype(F32))


def mul_fine(left, right):
    left_high, left_low = halves(left)
    right_high, right_low = halves(right)
    return mul(left_high, right_high) + (mul(left_high, right_low) + mul(left_low, right_high))


def sigmoid(value):
    return 1.0 / (1.0 + jnp.exp(-value))


def softplus(value):
    return jnp.maximum(value, 0.0) + jnp.log1p(jnp.exp(-jnp.abs(value)))


def span_masks():
    rows = lax.broadcasted_iota(jnp.int32, (SPAN, SPAN), 0)
    cols = lax.broadcasted_iota(jnp.int32, (SPAN, SPAN), 1)
    same = (rows // BLOCK) == (cols // BLOCK)
    return rows, cols, same


def decay_terms(raw, rate, bias, masks):
    rows, cols, same = masks
    causal = same & (rows >= cols)
    column = -jnp.exp(rate) * softplus(raw + bias)
    line = jnp.sum(jnp.where(rows == cols, column, 0.0), axis=0, keepdims=True)
    running = jnp.sum(jnp.where(causal, line, 0.0), axis=1, keepdims=True)
    running_line = jnp.sum(jnp.where(same & (rows <= cols), column, 0.0), axis=0, keepdims=True)
    final = jnp.sum(jnp.where(same, line, 0.0), axis=1, keepdims=True)
    ratio = jnp.where(causal, jnp.exp(jnp.where(causal, running - running_line, 0.0)), 0.0)
    return column, running, final, ratio


def unit_inverse(coupling, masks):
    rows, cols, same = masks
    inverse = jnp.where(rows == cols, 1.0, 0.0) - jnp.where(
        (rows // 2 == cols // 2), coupling, 0.0
    )
    width = 2
    while width < BLOCK:
        inner = (rows // (2 * width) == cols // (2 * width)) & (rows // width != cols // width)
        part = jnp.where(inner, coupling, 0.0)
        inverse = inverse - mul_fine(mul_fine(inverse, part), inverse)
        width = width * 2
    return inverse


def second_start(lengths_ref):
    return (lengths_ref[0, 0] + BLOCK - 1) // BLOCK * BLOCK


def held_rows(order_ref, index):
    half = index % 2
    return pl.multiple_of(order_ref[index // 2] * PART + half * BLOCK, BLOCK)


def part_rows(order_ref, index):
    return pl.ds(pl.multiple_of(order_ref[index] * PART, PART), PART)


def past_rows(order_ref, index):
    return pl.multiple_of(held_rows(order_ref, jnp.maximum(index - 1, 0)) + BLOCK - 8, 8)


def row_limit(lengths_ref, start, base, count):
    place = lax.broadcasted_iota(jnp.int32, (count, 1), 0) + base
    limit = jnp.where(place >= start, start + lengths_ref[0, 1], lengths_ref[0, 0])
    return place < limit


def front_kernel(
    lengths_ref,
    order_ref,
    rates_ref,
    proj_ref,
    taps_ref,
    query_ref,
    key_ref,
    value_ref,
    raw_ref,
    inverse_ref,
    reach_ref,
    base_ref,
    tail_ref,
    score_ref,
    growth_ref,
):
    start = second_start(lengths_ref)
    rate = rates_ref[0, 0]
    bias = rates_ref[1, 0]

    def front(index, carry):
        base = pl.multiple_of(index * BLOCK, BLOCK)
        held = held_rows(order_ref, index)
        before = past_rows(order_ref, index)
        broken = (base == 0) | (base == start)
        raw_ref[pl.ds(base, BLOCK), :] = proj_ref[pl.ds(held, BLOCK), FRONT:WIDE]
        for at in range(0, FRONT, DK):
            here = slice(at, at + DK)
            taps = taps_ref[:, here]
            halo = jnp.where(broken, 0.0, proj_ref[pl.ds(before, 8), here])
            block = proj_ref[pl.ds(held, BLOCK), here]
            joined = jnp.concatenate([halo, block], axis=0)
            conv = block * taps[0:1]
            for offset in range(1, 4):
                conv = conv + pltpu.roll(joined, offset, 0)[8:] * taps[offset : offset + 1]
            act = conv * sigmoid(conv)
            if at >= 2 * DK:
                value_ref[pl.ds(base, BLOCK), at - 2 * DK : at - DK] = low(act)
            else:
                inv = lax.rsqrt(jnp.sum(act * act, axis=1, keepdims=True) + 1e-06)
                if at == 0:
                    query_ref[pl.ds(base, BLOCK), :] = low(act * inv * DK ** (-0.5))
                else:
                    key_ref[pl.ds(base, BLOCK), :] = low(act * inv)
        return carry

    lax.fori_loop(0, BLOCKS, front, 0)

    masks = span_masks()
    rows, cols, same = masks
    strict = same & (rows > cols)
    lane = lax.broadcasted_iota(jnp.int32, (SPAN, 128), 1)
    for span in range(SPANS):
        at = slice(span * SPAN, (span + 1) * SPAN)
        raw = raw_ref[at, :]
        beta = sigmoid(raw[:, 0:1])
        _, running, final, ratio = decay_terms(raw[:, 1:2], rate, bias, masks)
        growth = jnp.exp(running)
        key = key_ref[at, :]
        coupling = jnp.where(strict, beta * mul_nt(key, key) * ratio, 0.0)
        inverse = low(unit_inverse(coupling, masks))
        inverse_ref[at, :] = inverse
        key_wide = key.astype(F32)
        base_ref[at, :] = mul(inverse, low(beta * value_ref[at, :].astype(F32)))
        reach_ref[at, :] = low(mul(inverse, low(beta * growth * key_wide)))
        tail_ref[at, :] = low(jnp.exp(final - running) * key_wide)
        score_ref[at, :] = low(mul_nt(query_ref[at, :], key) * ratio)
        growth_ref[at, :] = jnp.where(lane == 0, growth, jnp.exp(final))


def chain_kernel(
    lengths_ref,
    order_ref,
    query_ref,
    reach_ref,
    base_ref,
    tail_ref,
    score_ref,
    growth_ref,
    gate_ref,
    gain_ref,
    gated_ref,
    state_ref,
    fresh_ref,
    out_ref,
    carry_ref,
):
    start = second_start(lengths_ref)
    carry_ref[...] = jnp.zeros_like(carry_ref)
    for index in range(BLOCKS):
        at = slice(index * BLOCK, (index + 1) * BLOCK)
        held = jnp.where(start == index * BLOCK, 0.0, carry_ref[...])
        state = low(held)
        state_ref[index] = state
        both = mul(jnp.concatenate([reach_ref[at, :], query_ref[at, :]], axis=0), state)
        fresh = low(base_ref[at, :] - both[:BLOCK])
        fresh_ref[at, :] = fresh
        out_ref[at, :] = growth_ref[at, 0:1] * both[BLOCK:]
        if index + 1 < BLOCKS:
            final = growth_ref[index * BLOCK : index * BLOCK + 1, 1:2]
            carry_ref[...] = final * held + mul_tn(tail_ref[at, :], fresh)

    gain = gain_ref[...]
    for part in range(TOTAL // PART):
        span = part * PART // SPAN
        here = slice(part * PART, (part + 1) * PART)
        out = out_ref[here, :] + mul(score_ref[here, :], fresh_ref[span * SPAN : (span + 1) * SPAN, :])
        out = jnp.where(row_limit(lengths_ref, start, part * PART, PART), out, 0.0)
        out_ref[here, :] = out
        inv = lax.rsqrt(jnp.mean(out * out, axis=1, keepdims=True) + 1e-06)
        held = part_rows(order_ref, part)
        gate = gate_ref[held, :]
        gated_ref[held, :] = low(out * inv * gain * (gate * sigmoid(gate)))


def gate_back_kernel(
    lengths_ref,
    order_ref,
    grad_ref,
    gate_ref,
    gain_ref,
    out_ref,
    dgate_ref,
    dout_ref,
    dgain_ref,
):
    start = second_start(lengths_ref)
    gain = gain_ref[...]
    dgain = jnp.zeros((1, DV), F32)
    for part in range(TOTAL // PART):
        here = slice(part * PART, (part + 1) * PART)
        held = part_rows(order_ref, part)
        out = out_ref[here, :]
        gate = gate_ref[held, :]
        grad = grad_ref[held, :]
        inv = lax.rsqrt(jnp.mean(out * out, axis=1, keepdims=True) + 1e-06)
        sig = sigmoid(gate)
        swish = gate * sig
        unit = out * inv
        pulled = grad * unit
        dgate_ref[held, :] = low(pulled * gain * (sig * (1.0 + gate * (1.0 - sig))))
        dgain = dgain + jnp.sum(pulled * swish, axis=0, keepdims=True)
        inner = grad * swish * gain
        dout = inv * (inner - unit * jnp.mean(inner * unit, axis=1, keepdims=True))
        dout_ref[here, :] = low(
            jnp.where(row_limit(lengths_ref, start, part * PART, PART), dout, 0.0)
        )
    dgain_ref[...] = dgain


def back_kernel(
    lengths_ref,
    order_ref,
    rates_ref,
    proj_ref,
    taps_ref,
    dout_ref,
    raw_ref,
    query_ref,
    key_ref,
    value_ref,
    state_ref,
    inverse_ref,
    reach_ref,
    fresh_ref,
    dproj_ref,
    dtaps_ref,
    drates_ref,
    dfresh_ref,
    dstate_ref,
    carry_ref,
    dq_ref,
    dk_ref,
    dv_ref,
    halo_ref,
):
    start = second_start(lengths_ref)
    rate = rates_ref[0, 0]
    bias = rates_ref[1, 0]
    masks = span_masks()
    rows, cols, same = masks
    causal = same & (rows >= cols)
    strict = same & (rows > cols)

    kept = []
    for span in range(SPANS):
        at = slice(span * SPAN, (span + 1) * SPAN)
        dout = dout_ref[at, :]
        raw = raw_ref[at, :]
        beta = sigmoid(raw[:, 0:1])
        column, running, final, ratio = decay_terms(raw[:, 1:2], rate, bias, masks)
        growth = jnp.exp(running)
        tail = jnp.exp(final - running)
        key = key_ref[at, :]
        score = mul_nt(query_ref[at, :], key) * ratio
        dfresh_ref[at, :] = mul_tn(low(score), dout)
        dscore = jnp.where(causal, mul_nt(dout, fresh_ref[at, :]), 0.0)
        tailed = low(tail * key.astype(F32))
        kept.append((beta, column, growth, final, tail, ratio, score, dscore, tailed))

    carry_ref[...] = jnp.zeros_like(carry_ref)
    ends = [None] * BLOCKS
    for index in reversed(range(BLOCKS)):
        at = slice(index * BLOCK, (index + 1) * BLOCK)
        low_at = index * BLOCK % SPAN
        inner = slice(low_at, low_at + BLOCK)
        beta, column, growth, final, tail, ratio, score, dscore, tailed = kept[index * BLOCK // SPAN]
        held = carry_ref[...]
        dstate = low(held)
        dstate_ref[index] = dstate
        dfresh = low(dfresh_ref[at, :] + mul(tailed[inner], dstate))
        dfresh_ref[at, :] = dfresh.astype(F32)
        scale = jnp.exp(final[low_at : low_at + 1])
        if index > 0:
            left = jnp.concatenate(
                [low(query_ref[at, :].astype(F32) * growth[inner]), -reach_ref[at, :]], axis=0
            )
            right = jnp.concatenate([dout_ref[at, :], dfresh], axis=0)
            carry_ref[...] = jnp.where(
                start == index * BLOCK, 0.0, scale * held + mul_tn(left, right)
            )
        ends[index] = scale * jnp.sum(
            jnp.sum(held * state_ref[index].astype(F32), axis=0, keepdims=True), axis=1, keepdims=True
        )

    drate = jnp.zeros((1, 1), F32)
    dbias = jnp.zeros((1, 1), F32)
    steps = SPAN // BLOCK
    for span in range(SPANS):
        at = slice(span * SPAN, (span + 1) * SPAN)
        beta, column, growth, final, tail, ratio, score, dscore, tailed = kept[span]
        query = query_ref[at, :]
        key = key_ref[at, :]
        key_wide = key.astype(F32)
        dright = mul_tn(inverse_ref[at, :], low(dfresh_ref[at, :]))
        dright_low = low(dright)
        dcouple = jnp.where(strict, -mul_nt(dright_low, fresh_ref[at, :]), 0.0)
        cross = mul_nt(key, key) * ratio
        weighted = dcouple * cross
        dbeta = jnp.sum(weighted, axis=1, keepdims=True)
        ratio_grad = dscore * score + weighted * beta
        dintersect = low(dcouple * beta * ratio)
        dscored = low(dscore * ratio)
        dquery = mul(dscored, key)
        dkey = mul_tn(dscored, query) + mul(dintersect, key) + mul_tn(dintersect, key)
        pieces = [[], [], []]
        for step in range(steps):
            index = span * steps + step
            here = slice(index * BLOCK, (index + 1) * BLOCK)
            joined = jnp.concatenate(
                [dout_ref[here, :], dright_low[step * BLOCK : (step + 1) * BLOCK]], axis=0
            )
            back = mul_nt(joined, state_ref[index])
            pieces[0].append(back[:BLOCK])
            pieces[1].append(back[BLOCK:])
            pieces[2].append(mul_nt(fresh_ref[here, :], dstate_ref[index]))
        out_back, right_back, tail_back = [jnp.concatenate(piece, axis=0) for piece in pieces]
        dquery = dquery + growth * out_back
        read = jnp.sum(key_wide * right_back, axis=1, keepdims=True)
        dkey = dkey - (beta * growth) * right_back + tail * tail_back
        dbeta = (
            dbeta
            + jnp.sum(dright * value_ref[at, :].astype(F32), axis=1, keepdims=True)
            - growth * read
        )
        dgrowth = jnp.sum(query.astype(F32) * out_back, axis=1, keepdims=True) - beta * read
        dtail = tail * jnp.sum(key_wide * tail_back, axis=1, keepdims=True)
        flat = jnp.sum(
            jnp.where(rows == cols, jnp.sum(ratio_grad, axis=0, keepdims=True), 0.0),
            axis=1,
            keepdims=True,
        )
        drunning = growth * dgrowth + jnp.sum(ratio_grad, axis=1, keepdims=True) - flat - dtail
        line = jnp.sum(jnp.where(rows == cols, drunning, 0.0), axis=0, keepdims=True)
        tail_line = jnp.sum(jnp.where(rows == cols, dtail, 0.0), axis=0, keepdims=True)
        ending = jnp.concatenate(
            [jnp.broadcast_to(ends[span * steps + step], (BLOCK, 1)) for step in range(steps)],
            axis=0,
        )
        dlog = (
            jnp.sum(jnp.where(same & (rows <= cols), line, 0.0), axis=1, keepdims=True)
            + jnp.sum(jnp.where(same, tail_line, 0.0), axis=1, keepdims=True)
            + ending
        )
        raw = raw_ref[at, :]
        ddecay = -jnp.exp(rate) * dlog * sigmoid(raw[:, 1:2] + bias)
        drate = drate + jnp.sum(dlog * column, axis=0, keepdims=True)
        dbias = dbias + jnp.sum(ddecay, axis=0, keepdims=True)
        dbeta = dbeta * beta * (1.0 - beta)
        lane = lax.broadcasted_iota(jnp.int32, (SPAN, 128), 1)
        draw = low(jnp.where(lane == 0, dbeta, jnp.where(lane == 1, ddecay, 0.0)))
        for half in range(SPAN // PART):
            held = part_rows(order_ref, span * (SPAN // PART) + half)
            dproj_ref[held, FRONT:WIDE] = draw[half * PART : (half + 1) * PART]
        dq_ref[at, :] = low(dquery)
        dk_ref[at, :] = low(dkey)
        dv_ref[at, :] = low(beta * dright)
    lane = lax.broadcasted_iota(jnp.int32, (8, 128), 1)
    drates_ref[...] = jnp.where(lane == 0, drate, jnp.where(lane == 1, dbias, 0.0))

    dtaps_ref[...] = jnp.zeros_like(dtaps_ref)
    halo_ref[...] = jnp.zeros_like(halo_ref)

    def back(step, carry):
        index = BLOCKS - 1 - step
        base = pl.multiple_of(index * BLOCK, BLOCK)
        held = held_rows(order_ref, index)
        before = past_rows(order_ref, index)
        broken = (base == 0) | (base == start)
        ended = (base + BLOCK == TOTAL) | (base + BLOCK == start)
        for at in range(0, FRONT, DK):
            here = slice(at, at + DK)
            taps = taps_ref[:, here]
            halo = jnp.where(broken, 0.0, proj_ref[pl.ds(before, 8), here])
            block = proj_ref[pl.ds(held, BLOCK), here]
            joined = jnp.concatenate([halo, block], axis=0)
            shifted = [block] + [pltpu.roll(joined, offset, 0)[8:] for offset in range(1, 4)]
            conv = shifted[0] * taps[0:1]
            for offset in range(1, 4):
                conv = conv + shifted[offset] * taps[offset : offset + 1]
            sig = sigmoid(conv)
            if at >= 2 * DK:
                dact = dv_ref[pl.ds(base, BLOCK), at - 2 * DK : at - DK].astype(F32)
            else:
                act = conv * sig
                given = (dq_ref if at == 0 else dk_ref)[pl.ds(base, BLOCK), :].astype(F32)
                inv = lax.rsqrt(jnp.sum(act * act, axis=1, keepdims=True) + 1e-06)
                along = jnp.sum(act * given, axis=1, keepdims=True)
                dact = inv * (given - act * (inv * inv * along))
                if at == 0:
                    dact = dact * DK ** (-0.5)
            dconv = dact * (sig * (1.0 + conv * (1.0 - sig)))
            after = jnp.where(ended, 0.0, halo_ref[:, here])
            halo_ref[:, here] = dconv[:8]
            trailing = jnp.concatenate([dconv, after], axis=0)
            dblock = dconv * taps[0:1]
            for offset in range(1, 4):
                moved = pltpu.roll(trailing, BLOCK + 8 - offset, 0)[:BLOCK]
                dblock = dblock + moved * taps[offset : offset + 1]
            dproj_ref[pl.ds(held, BLOCK), here] = low(dblock)
            for offset in range(4):
                dtaps_ref[offset : offset + 1, here] += jnp.sum(
                    dconv * shifted[offset], axis=0, keepdims=True
                )
        return carry

    lax.fori_loop(0, BLOCKS, back, 0)


def run_kernel(kernel, name, scalars, arrays, results, scratch, cost):
    return pl.pallas_call(
        kernel,
        out_shape=tuple(jax.ShapeDtypeStruct(shape, kind) for shape, kind in results),
        in_specs=[pl.BlockSpec(memory_space=SMEM)] * len(scalars)
        + [pl.BlockSpec(memory_space=VMEM)] * len(arrays),
        out_specs=tuple([pl.BlockSpec(memory_space=VMEM)] * len(results)),
        scratch_shapes=[pltpu.VMEM(shape, kind) for shape, kind in scratch],
        compiler_params=pltpu.CompilerParams(vmem_limit_bytes=LIMIT),
        cost_estimate=pl.CostEstimate(
            flops=cost * 1_000_000_000, bytes_accessed=8_000_000, transcendentals=1_000_000
        ),
        name=name,
    )(*scalars, *arrays)


def front_call(lengths, order, rates, proj, taps):
    results = (
        ((TOTAL, DK), BF16),
        ((TOTAL, DK), BF16),
        ((TOTAL, DV), BF16),
        ((TOTAL, 128), F32),
        ((TOTAL, SPAN), BF16),
        ((TOTAL, DK), BF16),
        ((TOTAL, DV), F32),
        ((TOTAL, DK), BF16),
        ((TOTAL, SPAN), BF16),
        ((TOTAL, 128), F32),
    )
    return run_kernel(
        front_kernel, "mixer_front", (lengths, order, rates), (proj, taps), results, (), 12
    )


def chain_call(lengths, order, query, reach, base, tail, score, growth, gate, gain):
    results = (
        ((TOTAL, DV), BF16),
        ((BLOCKS, DK, DV), BF16),
        ((TOTAL, DV), BF16),
        ((TOTAL, DV), F32),
    )
    return run_kernel(
        chain_kernel,
        "mixer_chain",
        (lengths, order),
        (query, reach, base, tail, score, growth, gate, gain),
        results,
        (((DK, DV), F32),),
        12,
    )


def gate_back_call(lengths, order, grad, gate, gain, out):
    results = (((TOTAL, DV), BF16), ((TOTAL, DV), BF16), ((1, DV), F32))
    return run_kernel(
        gate_back_kernel, "gate_back", (lengths, order), (grad, gate, gain, out), results, (), 4
    )


def back_call(lengths, order, rates, arrays):
    results = (((TOTAL, WIDE), BF16), ((4, FRONT), F32), ((8, 128), F32))
    scratch = (
        ((TOTAL, DV), F32),
        ((BLOCKS, DK, DV), BF16),
        ((DK, DV), F32),
        ((TOTAL, DK), BF16),
        ((TOTAL, DK), BF16),
        ((TOTAL, DV), BF16),
        ((8, FRONT), F32),
    )
    return run_kernel(
        back_kernel, "mixer_back", (lengths, order, rates), arrays, results, scratch, 50
    )


def plain_product(left, right):
    return jnp.dot(left, right, preferred_element_type=F32)


def transposed_product(left, right):
    return lax.dot_general(left, right, (((0,), (0,)), ((), ())), preferred_element_type=F32)


def product_back(grad, weight):
    return lax.dot_general(grad, weight, (((1,), (1,)), ((), ())), preferred_element_type=F32)


def plain_scale(value, gain):
    return value * lax.rsqrt(jnp.mean(value * value, axis=-1, keepdims=True) + 1e-06) * gain


class Ring:
    def __init__(self, count):
        self.count = count
        self.circle = count % 2 == 0 and 4 <= count <= 16
        if self.circle:
            self.order = list(range(0, count, 2)) + list(range(count - 1, 0, -2))
        else:
            self.order = list(range(count))
        place = [self.order.index(i) for i in range(count)]
        here = lax.axis_index("dp")
        if self.circle:
            ahead = [[self.order[(place[i] + d) % count] for d in range(count)] for i in range(count)]
            behind = [[(place[j] - place[i]) % count for j in range(count)] for i in range(count)]
            self.ahead = jnp.array(ahead, jnp.int32)[here]
            self.behind = jnp.array(behind, jnp.int32)[here]

    def step(self, value, forward):
        pairs = [(self.order[i], self.order[(i + 1) % self.count]) for i in range(self.count)]
        if not forward:
            pairs = [(b, a) for a, b in pairs]
        return lax.ppermute(value, "dp", pairs)

    def gather(self, parts):
        if not self.circle:
            whole = [lax.all_gather(part, "dp", axis=0) for part in parts]
            return [[one[d] for d in range(self.count)] for one in whole]
        middle = self.count // 2
        result = []
        for part in parts:
            pieces = [None] * self.count
            pieces[0] = part
            up = down = part
            for hop in range(1, middle):
                up = self.step(up, True)
                down = self.step(down, False)
                pieces[self.count - hop] = up
                pieces[hop] = down
            cut = part.shape[0] // 2
            pieces[middle] = jnp.concatenate(
                [self.step(up[:cut], True), self.step(down[cut:], False)], axis=0
            )
            result.append(pieces)
        return result

    def scatter_sum(self, pieces):
        kind = pieces[0].dtype
        if not self.circle:
            whole = jnp.stack(pieces)
            return lax.psum_scatter(whole, "dp", scatter_dimension=0, tiled=False).astype(F32)
        middle = self.count // 2
        cut = pieces[0].shape[0] // 2
        up = self.step(pieces[middle][:cut], True).astype(F32)
        down = self.step(pieces[middle][cut:], False).astype(F32)
        for hop in range(middle - 1, 0, -1):
            ahead = pieces[hop].astype(F32)
            back = pieces[self.count - hop].astype(F32)
            if hop == middle - 1:
                ahead = jnp.concatenate([ahead[:cut] + up, ahead[cut:]], axis=0)
                back = jnp.concatenate([back[:cut], back[cut:] + down], axis=0)
            else:
                ahead = ahead + up
                back = back + down
            up = self.step(ahead.astype(kind), True).astype(F32)
            down = self.step(back.astype(kind), False).astype(F32)
        return pieces[0].astype(F32) + up + down

    def to_ahead(self, value):
        return self.reorder(value, "ahead")

    def to_mesh(self, value):
        return self.reorder(value, "behind")

    def reorder(self, value, which):
        if not self.circle:
            return value
        index = getattr(self, which)
        width = value.shape[1] // self.count
        return jnp.concatenate(
            [
                lax.dynamic_slice_in_dim(value, index[d] * width, width, axis=1)
                for d in range(self.count)
            ],
            axis=1,
        )


def swap(value, distance):
    count = lax.axis_size("tensor")
    return lax.ppermute(value, "tensor", [(i, i ^ distance) for i in range(count)])


def team_gather(value):
    other = swap(value, 2)
    near = swap(value, 1)
    far = swap(other, 1)
    return jnp.concatenate([value, other, near, far], axis=0)


def team_sum_rows(value):
    half = value.shape[0] // 2
    got = swap(value[half:], 1)
    both = value[:half].astype(F32) + got.astype(F32)
    quarter = half // 2
    return both[:quarter] + swap(low(both[quarter:]), 2).astype(F32)


def team_sum(value):
    value = value + swap(value, 1)
    return value + swap(value, 2)


def local(
    tokens,
    lengths,
    cotangent,
    norm_gain,
    query_weight,
    key_weight,
    value_weight,
    gate_weight,
    beta_weight,
    decay_weight,
    query_conv,
    key_conv,
    value_conv,
    decay_params,
    head_gain,
    out_weight,
    ffn_gain,
    ffn_gate,
    ffn_up,
    ffn_down,
):
    count = lax.axis_size("dp")
    team = lax.axis_size("tensor")
    ring = Ring(count)
    place = lax.axis_index("tensor")
    swapped = [[[0, 2, 1, 3][i ^ t] for i in range(team)] for t in range(team)]
    order = jnp.array(swapped, jnp.int32)[place]
    share = norm_gain.shape[0]
    narrow = head_gain.shape[0]

    channels = jnp.concatenate([query_conv, key_conv, value_conv], axis=1)
    pack = jnp.concatenate(
        [
            beta_weight,
            decay_weight,
            norm_gain[:, None],
            ffn_gain[:, None],
            channels.T,
            jnp.pad(head_gain, (0, share - narrow))[:, None],
            jnp.zeros((share, 119), BF16),
        ],
        axis=1,
    )
    entry = jnp.concatenate([query_weight, key_weight, value_weight, pack], axis=1)
    rows_here = tokens.shape[0]
    tokens = ring.to_ahead(tokens)
    cotangent = ring.to_ahead(cotangent)
    both_whole = team_gather(jnp.concatenate([tokens, cotangent], axis=1))
    width = tokens.shape[1]
    tokens_whole = both_whole[:, :width]
    down_grad = both_whole[:, width:]

    (entry_pieces,) = ring.gather([entry])
    entry_whole = jnp.concatenate(entry_pieces, axis=0)
    gate_pieces, out_pieces = ring.gather([gate_weight, out_weight])
    gate_whole = jnp.concatenate(gate_pieces, axis=0)
    out_whole = jnp.concatenate(out_pieces, axis=1)
    wide_pieces, down_pieces = ring.gather(
        [jnp.concatenate([ffn_gate, ffn_up], axis=1), ffn_down]
    )
    wide_whole = jnp.concatenate(wide_pieces, axis=0)
    down_whole = jnp.concatenate(down_pieces, axis=1)

    pack_whole = entry_whole[:, FRONT:WIDE]
    norm_whole = pack_whole[:, 2].astype(F32)
    ffn_gain_whole = pack_whole[:, 3].astype(F32)
    small = pack_whole[:, 4:9].astype(F32).reshape(count, share, 5)
    if ring.circle:
        small = small[ring.behind]
    narrow_q = query_conv.shape[1]
    cuts = (0, narrow_q, 2 * narrow_q, share)
    taps = jnp.concatenate(
        [small[:, a:b, :4].reshape(-1, 4) for a, b in zip(cuts[:-1], cuts[1:])], axis=0
    ).T
    gains = small[:, :narrow, 4].reshape(1, DV)

    token_rows = tokens.astype(F32)
    all_rows = tokens_whole.astype(F32)
    unit_rows = all_rows * lax.rsqrt(jnp.mean(all_rows * all_rows, axis=-1, keepdims=True) + 1e-06)
    mixer_input = (unit_rows * norm_whole).astype(BF16)
    proj = plain_product(mixer_input, entry_whole)
    (
        query,
        key,
        value,
        raw,
        inverse,
        reach,
        base,
        tail,
        score,
        growth,
    ) = front_call(lengths, order, decay_params, proj, taps)
    gate_proj = plain_product(mixer_input, gate_whole)
    gated, state, fresh, out = chain_call(
        lengths, order, query, reach, base, tail, score, growth, gate_proj, gains
    )
    mixed = team_sum_rows(plain_product(gated, out_whole).astype(BF16))
    middle = token_rows + mixed
    second_norm, second_pull = jax.vjp(plain_scale, middle, ffn_gain_whole)
    ffn_input = team_gather(second_norm.astype(BF16))
    hidden = wide_whole.shape[1] // 2
    acts = plain_product(ffn_input, wide_whole)
    gate_act = acts[:, :hidden]
    up_act = acts[:, hidden:]
    sigmoid_gate = jax.nn.sigmoid(gate_act)
    swish = gate_act * sigmoid_gate
    product_rows = (swish * up_act).astype(BF16)
    ffn_out = team_sum_rows(plain_product(product_rows, down_whole).astype(BF16))
    block_out = ring.to_mesh((middle + ffn_out).astype(BF16))

    grad_product = product_back(down_grad, down_whole)
    grad_gate_act = (
        grad_product * up_act * sigmoid_gate * (1.0 + gate_act * (1.0 - sigmoid_gate))
    ).astype(BF16)
    grad_up_act = (grad_product * swish).astype(BF16)
    grad_acts = jnp.concatenate([grad_gate_act, grad_up_act], axis=1)
    ffn_input_part = product_back(grad_acts, wide_whole)
    grad_second = team_sum_rows(ffn_input_part.astype(BF16))
    grad_middle_norm, grad_ffn_gain = second_pull(grad_second)
    grad_middle = cotangent.astype(F32) + grad_middle_norm
    grad_mixed = team_gather(grad_middle.astype(BF16))

    grad_wide = transposed_product(ffn_input, grad_acts).astype(BF16)
    grad_down = transposed_product(product_rows, down_grad).astype(BF16)

    def by_rows(value):
        return [value[d * share : (d + 1) * share] for d in range(count)]

    def by_cols(value):
        return [value[:, d * share : (d + 1) * share] for d in range(count)]

    wide_sum = ring.scatter_sum(by_rows(grad_wide))
    down_sum = ring.scatter_sum(by_cols(grad_down))

    grad_out = transposed_product(gated, grad_mixed).astype(BF16)
    out_sum = ring.scatter_sum(by_cols(grad_out))
    grad_gated = product_back(grad_mixed, out_whole)
    dgate, dout, dgain = gate_back_call(lengths, order, grad_gated, gate_proj, gains, out)
    grad_gate = transposed_product(mixer_input, dgate).astype(BF16)
    gate_sum = ring.scatter_sum(by_rows(grad_gate))
    dproj, dtaps, drates = back_call(
        lengths,
        order,
        decay_params,
        (proj, taps, dout, raw, query, key, value, state, inverse, reach, fresh),
    )
    grad_entry = transposed_product(mixer_input, dproj)
    entry_sum = ring.scatter_sum(by_rows(low(grad_entry[:, :FRONT])))
    input_part = product_back(dproj, entry_whole) + product_back(dgate, gate_whole)
    grad_first = team_sum_rows(input_part.astype(BF16))
    first_unit = lax.rsqrt(jnp.mean(token_rows * token_rows, axis=-1, keepdims=True) + 1e-06)
    pulled = grad_first * norm_whole
    grad_tokens_norm = first_unit * pulled - token_rows * (
        first_unit * first_unit * first_unit * jnp.mean(pulled * token_rows, axis=-1, keepdims=True)
    )
    tokens_grad = ring.to_mesh(grad_middle + grad_tokens_norm)
    grad_norm_gain = jnp.sum(input_part * unit_rows, axis=0)

    gain_sums = team_sum(jnp.stack([grad_norm_gain, grad_ffn_gain], axis=1))
    channel_parts = [
        dtaps[:, a * count : b * count].T.reshape(count, b - a, 4)
        for a, b in zip(cuts[:-1], cuts[1:])
    ]
    channel_grads = jnp.concatenate(
        [
            jnp.concatenate(channel_parts, axis=1),
            jnp.pad(dgain.reshape(count, narrow, 1), ((0, 0), (0, share - narrow), (0, 0))),
        ],
        axis=2,
    )
    if ring.circle:
        channel_grads = channel_grads[ring.ahead]
    pack_grad = jnp.concatenate(
        [
            grad_entry[:, FRONT : FRONT + 2],
            gain_sums,
            channel_grads.reshape(count * share, 5),
            jnp.broadcast_to(drates[0:1, 0:2], (count * share, 2)),
            jnp.zeros((count * share, 117), F32),
        ],
        axis=1,
    )
    pack_sum = ring.scatter_sum(by_rows(pack_grad))
    tap_sum = pack_sum[:, 4:8].T
    return (
        block_out,
        tokens_grad,
        pack_sum[:, 2],
        entry_sum[:, :DK],
        entry_sum[:, DK : 2 * DK],
        entry_sum[:, 2 * DK :],
        gate_sum,
        pack_sum[:, 0:1],
        pack_sum[:, 1:2],
        tap_sum[:, cuts[0] : cuts[1]],
        tap_sum[:, cuts[1] : cuts[2]],
        tap_sum[:, cuts[2] : cuts[3]],
        pack_sum[0, 9:11][:, None],
        pack_sum[:narrow, 8],
        out_sum,
        pack_sum[:, 3],
        wide_sum[:, :hidden],
        wide_sum[:, hidden:],
        down_sum,
    )


def solution(mesh):
    rows = P(("dp", "tensor"), None)
    weight = P("dp", "tensor")
    channel = P(None, ("tensor", "dp"))
    down = P("tensor", "dp")
    return jax.shard_map(
        local,
        mesh=mesh,
        in_specs=(
            rows,
            P("dp", None),
            rows,
            P("dp"),
            weight,
            weight,
            weight,
            weight,
            weight,
            weight,
            channel,
            channel,
            channel,
            P(None, "tensor"),
            P(("tensor", "dp")),
            down,
            P("dp"),
            weight,
            weight,
            down,
        ),
        out_specs=(
            rows,
            rows,
            P("dp"),
            weight,
            weight,
            weight,
            weight,
            weight,
            weight,
            channel,
            channel,
            channel,
            P(None, "tensor"),
            P(("tensor", "dp")),
            down,
            P("dp"),
            weight,
            weight,
            down,
        ),
        check_vma=False,
    )
```

time: 2090 us -> 404 us (0.19)
  waiting for transfers between devices: 1030 us -> 104 us
  blocking collectives: 268 us -> 0 us
  matrix products: 292 us -> 30.7 us
  other arithmetic: 253 us -> 35.4 us
  local copies, waits for them, and re-layouts: 175 us -> 73.5 us
  starting transfers between devices: 10.1 us -> 105 us
  Pallas kernels: 0 us -> 36.6 us
  loops' own time: 23.4 us -> 0 us
    reduce_scatter x12 -> x0, waiting for transfers between devices: 623 us -> none  [the longest x1 75.7 us: local(): lax.psum_scatter(grad_ffn_up, 'dp', scatter_dimension=0, tiled=True)]
    unnamed x32 -> x0, waiting for transfers between devices: 236 us -> none
    dot_general x162 -> x5, matrix products: 226 us -> 11.6 us  [plain_product(): return jnp.dot(left, right, preferred_element_type=F32)]
    all_gather x9 -> x0, blocking collectives: 188 us -> none  [the longest x1 32 us: local(): lax.all_gather(key_weight, 'dp', axis=0, tiled=True)]
    all_gather x10 -> x0, waiting for transfers between devices: 169 us -> none  [the longest x1 45.9 us: local(): lax.all_gather(ffn_down, 'dp', axis=1, tiled=True)]
    ppermute x0 -> x107, starting transfers between devices: none -> 105 us  [the longest x88 94.1 us: step(): return lax.ppermute(value, 'dp', pairs)]
    ppermute x0 -> x107, waiting for transfers between devices: none -> 104 us  [the longest x88 97.4 us: step(): return lax.ppermute(value, 'dp', pairs)]
    another operation x93 -> x6, other arithmetic: 96.3 us -> 2.08 us  [the longest x48 85.9 us: block_step(): lax.linalg.triangular_solve(system, right_heads, left_side=True, lower=Tr...]
  transfers between devices with their start and end apart: 27 -> 107, of which waited for: 21 -> 40; matrix products, arithmetic and copies ran while one was open for 15% -> 29% of each run, Pallas kernels for 0% -> 5%
where the time goes in v1:
time: 404 us; the launch traced here: 398 us
  starting transfers between devices  105 us (26%)
  waiting for transfers between devices  104 us (26%)
  local copies, waits for them, and re-layouts  73.5 us (18%)
  Pallas kernels  36.6 us (9%)
  other arithmetic  35.4 us (9%)
  matrix products  30.7 us (8%)
  between operations  12.6 us (3%)
    ppermute x88, waiting for transfers between devices, step(): return lax.ppermute(value, 'dp', pairs)  97.4 us
    ppermute x88, starting transfers between devices, step(): return lax.ppermute(value, 'dp', pairs)  94.1 us
    pallas_call x4, Pallas kernels, run_kernel(): pl.pallas_call(kernel, out_shape=tuple((jax.ShapeDtypeStruct(shape, kind)...  36.6 us
    unnamed x173, local copies, waits for them, and re-layouts  36.1 us
    dot_general x5, matrix products, transposed_product(): lax.dot_general(left, right, (((0,), (0,)), ((), ())), preferred_element_...  11.8 us
    dot_general x5, matrix products, plain_product(): return jnp.dot(left, right, preferred_element_type=F32)  11.6 us
    ppermute x19, starting transfers between devices, swap(): lax.ppermute(value, 'tensor', [(i, i ^ distance) for i in range(count)])  10.6 us
  transfers between devices with their start and end apart: 107, of which 40 were waited for; matrix products, arithmetic and copies ran while one was open for 29% of the time, Pallas kernels for 5%

profile of v1, /device:TPU:0, one launch (start us, length us, event | category | flops | bytes accessed | tf_op | source)
XLA Modules:
  0.0 397.6 jit_solution(425676509411074795)
XLA Ops:
  0.7 3.0 collective-permute-start.11
  3.8 1.9 collective-permute-start.19
  11.3 1.9 collective-permute-start.3
  51.6 4.1 %collective-permute-done.16 = bf16[128,512]{1,0:T(8,128)(2,1)S(1)} collective-permute-done((bf16[128,512]{1,0:T(8,128)(2,1)S(1)}, bf16[128,512]{1,0:T(8,128)(2,1)S(1)}, u32[]{:S(2)}, u32[]{:S(2)}) %collective-permute-start.16) | collective-permute-done | bytes 131104 | tf_op jit(solution)/shard_map/ppermute | solution.py:577
  64.3 4.2 %collective-permute-done.17 = bf16[64,512]{1,0:T(8,128)(2,1)S(1)} collective-permute-done((bf16[64,512]{1,0:T(8,128)(2,1)S(1)}, bf16[64,512]{1,0:T(8,128)(2,1)S(1)}, u32[]{:S(2)}, u32[]{:S(2)}) %collective-permute-start.17) | collective-permute-done | bytes 65568 | tf_op jit(solution)/shard_map/ppermute | solution.py:577
  76.5 4.4 %collective-permute-done.8 = bf16[128,1152]{0,1:T(8,128)(2,1)S(1)} collective-permute-done((bf16[128,1152]{0,1:T(8,128)(2,1)S(1)}, bf16[128,1152]{0,1:T(8,128)(2,1)S(1)}, u32[]{:S(2)}, u32[]{:S(2)}) %collective-permute-start.8) | collective-permute-done | bytes 294944 | tf_op jit(solution)/shard_map/ppermute | solution.py:577
  81.6 1.8 collective-permute-start.10
  84.8 2.9 collective-permute-done.9
  88.6 3.9 concatenate.121
  94.9 1.8 pad_maximum_fusion
  97.2 3.0 fusion.37.proj_ref
  100.2 1.7 fusion.35.gate_ref
  101.9 11.4 %mixer_front.1 = (bf16[512,256]{1,0:T(8,128)(2,1)}, bf16[512,256]{1,0:T(8,128)(2,1)}, bf16[512,512]{1,0:T(8,128)(2,1)}, f32[512,128]{1,0:T(8,128)}, bf16[512,256...) custom-call(s32[1,2]{1,0:T(1,128)} %lengths_ref.7, ...), custom_call_target="tpu_custom_call" | custom-call | flops 12000000000 | bytes 8000000 | tf_op jit(solution)/shard_map/mixer_front/pallas_call | solution.py:467
  113.4 6.8 %mixer_chain.1 = (bf16[512,512]{1,0:T(8,128)(2,1)}, bf16[8,256,512]{2,1,0:T(8,128)(2,1)}, bf16[512,512]{1,0:T(8,128)(2,1)}, f32[512,512]{1,0:T(8,128)}) custom-call(s32[1,2]{1,0:T(1,128)} %lengths_ref.7, s32[4]{0:T(128)} %fusion.24.order_ref, bf16[512,256]{1,0:T(8,128)(2,1)} %get-tuple-element.39.query_ref, bf16[512,256]{1,0:T(8,128)(2,1)} %get-tuple-element.40.reach_ref, ...), custom_call_target="tpu_custom_call" | custom-call | flops 12000000000 | bytes 8000000 | tf_op jit(solution)/shard_map/mixer_chain/pallas_call | solution.py:467
  120.2 1.8 convolution_convert_fusion.6
  127.7 5.8 %collective-permute-done.32 = bf16[128,1408]{0,1:T(8,128)(2,1)S(1)} collective-permute-done((bf16[128,1408]{0,1:T(8,128)(2,1)S(1)}, bf16[128,1408]{0,1:T(8,128)(2,1)S(1)}, u32[]{:S(2)}, u32[]{:S(2)}) %collective-permute-start.32) | collective-permute-done | bytes 360480 | tf_op jit(solution)/shard_map/ppermute | solution.py:577
  147.7 2.1 collective-permute-done.41
  163.3 1.7 collective-permute-done.46
  170.6 6.7 %collective-permute-done.38 = bf16[64,1408]{0,1:T(8,128)(2,1)S(1)} collective-permute-done((bf16[64,1408]{0,1:T(8,128)(2,1)S(1)}, bf16[64,1408]{0,1:T(8,128)(2,1)S(1)}, u32[]{:S(2)}, u32[]{:S(2)}) %collective-permute-start.38) | collective-permute-done | bytes 180256 | tf_op jit(solution)/shard_map/ppermute | solution.py:577
  178.0 5.4 %concatenate.128 = bf16[1024,1408]{0,1:T(8,128)(2,1)} concatenate(bf16[128,1408]{0,1:T(8,128)(2,1)} %copy-done.18, bf16[128,1408]{0,1:T(8,128)(2,1)} %copy-done.20, bf16[128,1408]{0,1:T(8,128)(2,1)} %collective-permute-done.33, bf16[128,1408]{0,1:T(8,128)(2,1)S(1)} %collective-permute-done.34, bf16[64,1408]{0,1:T(8,128)(2,1)} %copy-done.22, ...), dimensions={0} | concatenate | bytes 5767168 | tf_op jit(solution)/shard_map/concatenate | solution.py:729
  183.4 4.1 %fusion.18 = f32[512,1408]{1,0:T(8,128)S(1)} fusion(bf16[1024,1408]{0,1:T(8,128)(2,1)} %concatenate.128, bf16[128,1024]{1,0:T(8,128)(2,1)} %collective-permute-done.31, bf16[128,1024]{1,0:T(8,128)(2,1)} %collective-permute-done.30, bf16[128,1024]{1,0:T(8,128)(2,1)} %collective-permute-done.29, bf16[128,1024]{1,0:T(8,128)(2,1)} %multiply_convert_fusion.3), kind=kOutput, calls=%fused_computation.97 | convolution fusion | flops 1480589312 | bytes 6815744 | tf_op jit(solution)/shard_map/dot_general | solution.py:542
  191.8 1.8 convolution_convert_fusion.2
  196.4 3.1 convolution_convert_fusion
  202.3 4.9 %collective-permute-done.91 = bf16[64,1408]{1,0:T(8,128)(2,1)S(1)} collective-permute-done((bf16[64,1408]{1,0:T(8,128)(2,1)S(1)}, bf16[64,1408]{1,0:T(8,128)(2,1)S(1)}, u32[]{:S(2)}, u32[]{:S(2)}) %collective-permute-start.91) | collective-permute-done | bytes 180256 | tf_op jit(solution)/shard_map/ppermute | solution.py:577
  211.2 2.8 collective-permute-done.104
  215.5 5.5 %collective-permute-done.101 = bf16[704,128]{1,0:T(8,128)(2,1)S(1)} collective-permute-done((bf16[704,128]{1,0:T(8,128)(2,1)S(1)}, bf16[704,128]{1,0:T(8,128)(2,1)S(1)}, u32[]{:S(2)}, u32[]{:S(2)}) %collective-permute-start.101) | collective-permute-done | bytes 180256 | tf_op jit(solution)/shard_map/ppermute | solution.py:577
  227.1 3.9 collective-permute-done.51
  231.0 2.4 collective-permute-start.106
  238.0 1.9 collective-permute-start.97
  241.9 7.0 %collective-permute-done.97 = bf16[128,1408]{1,0:T(8,128)(2,1)S(1)} collective-permute-done((bf16[128,1408]{1,0:T(8,128)(2,1)S(1)}, bf16[128,1408]{1,0:T(8,128)(2,1)S(1)}, u32[]{:S(2)}, u32[]{:S(2)}) %collective-permute-start.97) | collective-permute-done | bytes 360480 | tf_op jit(solution)/shard_map/ppermute | solution.py:577
  249.8 1.7 collective-permute-start.98
  251.5 1.8 fusion.17.grad_ref
  253.3 3.7 gate_back.1
  257.0 14.6 %mixer_back.1 = (bf16[512,1152]{1,0:T(8,128)(2,1)}, f32[4,1024]{1,0:T(4,128)}, f32[8,128]{1,0:T(8,128)}) custom-call(s32[1,2]{1,0:T(1,128)} %lengths_ref.7, s32[4]{0:T(128)} %fusion.24.order_ref, f32[2,1]{1,0:T(2,128)} %copy.104.rates_ref, f32[512,1152]{1,0:T(8,128)} %fusion.37.proj_ref, f32[4,1024]{1,0:T(4,128)} %maximum_bitcast_fusion.taps_ref, ...), custom_call_target="tpu_custom_call" | custom-call | flops 49999998976 | bytes 8000000 | tf_op jit(solution)/shard_map/mixer_back/pallas_call | solution.py:467
  275.0 5.2 %fusion.52 = (bf16[1024,1152]{1,0:T(8,128)(2,1)S(1)}, f32[1024,1152]{1,0:T(8,128)}) fusion(bf16[512,1152]{1,0:T(8,128)(2,1)S(1)} %copy-done.12, f32[1024]{0:T(1024)S(1)} %bitcast.100, f32[512]{0:T(512)S(1)} %add_rsqrt_fusion, bf16[512,2048]{1,0:T(8,128)(2,1)} %copy-done), kind=kOutput, calls=%fused_computation.248 | convolution fusion | flops 1211236352 | bytes 9312256 | tf_op jit(solution)/shard_map/dot_general | solution.py:546
  285.2 1.7 convolution_convert_fusion.4
  295.9 2.1 concatenate.138
  299.5 2.9 collective-permute-done.59
  302.4 1.7 collective-permute-start.79
  304.7 2.5 collective-permute-done.79
  307.2 1.7 collective-permute-start.87
  311.7 1.7 collective-permute-start.63
  316.5 4.0 %collective-permute-done.60 = f32[128,128]{0,1:T(8,128)S(1)} collective-permute-done((f32[128,128]{0,1:T(8,128)S(1)}, f32[128,128]{0,1:T(8,128)S(1)}, u32[]{:S(2)}, u32[]{:S(2)}) %collective-permute-start.60) | collective-permute-done | bytes 65568 | tf_op jit(solution)/shard_map/ppermute | solution.py:577
  320.6 1.8 collective-permute-start.71
  322.4 1.8 collective-permute-start.64
  328.0 2.6 collective-permute-done.61
  330.7 1.8 collective-permute-done.76
  332.5 1.8 collective-permute-start.65
  337.3 1.7 collective-permute-start.66
  341.9 1.7 collective-permute-start.80
  343.7 1.9 collective-permute-start.88
  351.2 1.9 copy.113
  354.0 1.7 collective-permute-start.72
  355.7 3.1 collective-permute-done.77
  360.0 2.1 collective-permute-start.81
  362.1 1.7 collective-permute-done.85
  364.9 2.1 collective-permute-start.89
  368.1 3.2 collective-permute-done.89
  372.2 2.1 collective-permute-start.82
  375.6 2.1 collective-permute-start.90
  383.0 1.7 collective-permute-start.73
  385.6 3.8 collective-permute-done.73
  389.4 1.7 collective-permute-start.74
  391.2 4.6 %collective-permute-done.74 = bf16[128,1024]{1,0:T(8,128)(2,1)S(1)} collective-permute-done((bf16[128,1024]{1,0:T(8,128)(2,1)S(1)}, bf16[128,1024]{1,0:T(8,128)(2,1)S(1)}, u32[]{:S(2)}, u32[]{:S(2)}) %collective-permute-start.74) | collective-permute-done | bytes 262176 | tf_op jit(solution)/shard_map/ppermute | solution.py:577
  (493 shorter events, 179.1 us)
Async XLA Ops:
  0.7 36.5 %collective-permute-start.11 = (bf16[128,512]{1,0:T(8,128)(2,1)}, bf16[128,512]{1,0:T(8,128)(2,1)S(1)}, u32[]{:S(2)}, u32[]{:S(2)}) collective-permute-start(bf16[128,512]{1,0:T(8,128)(2,1)} %param.30), channel_id=1, source_target_pairs={{8,0},{16,8},{24,16},{28,24},{20,28},{12,20},{4,12},{0,4},{9,1},{1... | collective-permute-start | bytes 393224 | tf_op jit(solution)/shard_map/ppermute | solution.py:577
  3.7 35.1 %collective-permute-start.14 = (bf16[128,512]{1,0:T(8,128)(2,1)}, bf16[128,512]{1,0:T(8,128)(2,1)S(1)}, u32[]{:S(2)}, u32[]{:S(2)}) collective-permute-start(bf16[128,512]{1,0:T(8,128)(2,1)} %param.30), channel_id=1, source_target_pairs={{0,8},{8,16},{16,24},{24,28},{28,20},{20,12},{12,4},{4,0},{1,9},{9... | collective-permute-start | bytes 393224 | tf_op jit(solution)/shard_map/ppermute | solution.py:577
  3.8 37.3 %collective-permute-start.19 = (bf16[512,128]{1,0:T(8,128)(2,1)}, bf16[512,128]{1,0:T(8,128)(2,1)S(1)}, u32[]{:S(2)}, u32[]{:S(2)}) collective-permute-start(bf16[512,128]{1,0:T(8,128)(2,1)} %param.38), channel_id=1, source_target_pairs={{8,0},{16,8},{24,16},{28,24},{20,28},{12,20},{4,12},{0,4},{9,1},{1... | collective-permute-start | bytes 393224 | tf_op jit(solution)/shard_map/ppermute | solution.py:577
  5.7 37.0 %collective-permute-start.22 = (bf16[512,128]{1,0:T(8,128)(2,1)}, bf16[512,128]{1,0:T(8,128)(2,1)S(1)}, u32[]{:S(2)}, u32[]{:S(2)}) collective-permute-start(bf16[512,128]{1,0:T(8,128)(2,1)} %param.38), channel_id=1, source_target_pairs={{0,8},{8,16},{16,24},{24,28},{28,20},{20,12},{12,4},{4,0},{1,9},{9... | collective-permute-start | bytes 393224 | tf_op jit(solution)/shard_map/ppermute | solution.py:577
  11.3 45.5 %collective-permute-start.3 = (bf16[128,1152]{0,1:T(8,128)(2,1)S(1)}, bf16[128,1152]{0,1:T(8,128)(2,1)S(1)}, u32[]{:S(2)}, u32[]{:S(2)}) collective-permute-start(bf16[128,1152]{0,1:T(8,128)(2,1)S(1)} %concatenate.120), channel_id=1, source_target_pairs={{8,0},{16,8},{24,16},{28,24},{20,28},{12,20},{4,12},{0,4},{9,1},{1... | collective-permute-start | bytes 884744 | tf_op jit(solution)/shard_map/ppermute | solution.py:577
  43.2 15.3 %collective-permute-start.6 = (bf16[128,1152]{0,1:T(8,128)(2,1)S(1)}, bf16[128,1152]{0,1:T(8,128)(2,1)S(1)}, u32[]{:S(2)}, u32[]{:S(2)}) collective-permute-start(bf16[128,1152]{0,1:T(8,128)(2,1)S(1)} %concatenate.120), channel_id=1, source_target_pairs={{0,8},{8,16},{16,24},{24,28},{28,20},{20,12},{12,4},{4,0},{1,9},{9... | collective-permute-start | bytes 884744 | tf_op jit(solution)/shard_map/ppermute | solution.py:577
  44.8 11.0 %collective-permute-start.16 = (bf16[128,512]{1,0:T(8,128)(2,1)S(1)}, bf16[128,512]{1,0:T(8,128)(2,1)S(1)}, u32[]{:S(2)}, u32[]{:S(2)}) collective-permute-start(bf16[128,512]{1,0:T(8,128)(2,1)S(1)} %collective-permute-done.15), channel_id=1, source_target_pairs={{0,8},{8,16},{16,24},{24,28},{28,20},{20,12},{12,4},{4,0},{1,9},{9... | collective-permute-start | bytes 393224 | tf_op jit(solution)/shard_map/ppermute | solution.py:577
  46.1 14.0 %collective-permute-start.13 = (bf16[128,512]{1,0:T(8,128)(2,1)}, bf16[128,512]{1,0:T(8,128)(2,1)S(1)}, u32[]{:S(2)}, u32[]{:S(2)}) collective-permute-start(bf16[128,512]{1,0:T(8,128)(2,1)} %collective-permute-done.12), channel_id=1, source_target_pairs={{8,0},{16,8},{24,16},{28,24},{20,28},{12,20},{4,12},{0,4},{9,1},{1... | collective-permute-start | bytes 393224 | tf_op jit(solution)/shard_map/ppermute | solution.py:577
  49.1 11.4 %collective-permute-start.21 = (bf16[512,128]{1,0:T(8,128)(2,1)S(1)}, bf16[512,128]{1,0:T(8,128)(2,1)S(1)}, u32[]{:S(2)}, u32[]{:S(2)}) collective-permute-start(bf16[512,128]{1,0:T(8,128)(2,1)S(1)} %collective-permute-done.20), channel_id=1, source_target_pairs={{8,0},{16,8},{24,16},{28,24},{20,28},{12,20},{4,12},{0,4},{9,1},{1... | collective-permute-start | bytes 393224 | tf_op jit(solution)/shard_map/ppermute | solution.py:577
  56.9 27.9 %collective-permute-start = (bf16[128,2048]{1,0:T(8,128)(2,1)}, bf16[128,2048]{1,0:T(8,128)(2,1)}, u32[]{:S(2)}, u32[]{:S(2)}) collective-permute-start(bf16[128,2048]{1,0:T(8,128)(2,1)} %constant_dynamic-update-slice_fusion.8), channel_id=1, source_target_pairs={{0,2},{1,3},{2,0},{3,1},{4,6},{5,7},{6,4},{7,5},{8,10},{9,11},{10,... | collective-permute-start | bytes 1572872 | tf_op jit(solution)/shard_map/ppermute | solution.py:645
  58.5 13.0 %collective-permute-start.4 = (bf16[128,1152]{0,1:T(8,128)(2,1)S(1)}, bf16[128,1152]{0,1:T(8,128)(2,1)S(1)}, u32[]{:S(2)}, u32[]{:S(2)}) collective-permute-start(bf16[128,1152]{0,1:T(8,128)(2,1)S(1)} %collective-permute-done.3), channel_id=1, source_target_pairs={{8,0},{16,8},{24,16},{28,24},{20,28},{12,20},{4,12},{0,4},{9,1},{1... | collective-permute-start | bytes 884744 | tf_op jit(solution)/shard_map/ppermute | solution.py:577
  60.1 13.0 %collective-permute-start.7 = (bf16[128,1152]{0,1:T(8,128)(2,1)S(1)}, bf16[128,1152]{0,1:T(8,128)(2,1)S(1)}, u32[]{:S(2)}, u32[]{:S(2)}) collective-permute-start(bf16[128,1152]{0,1:T(8,128)(2,1)S(1)} %collective-permute-done.6), channel_id=1, source_target_pairs={{0,8},{8,16},{16,24},{24,28},{28,20},{20,12},{12,4},{4,0},{1,9},{9... | collective-permute-start | bytes 884744 | tf_op jit(solution)/shard_map/ppermute | solution.py:577
  60.6 7.9 %collective-permute-start.17 = (bf16[64,512]{1,0:T(8,128)(2,1)S(1)}, bf16[64,512]{1,0:T(8,128)(2,1)S(1)}, u32[]{:S(2)}, u32[]{:S(2)}) collective-permute-start(bf16[64,512]{1,0:T(8,128)(2,1)S(1)} %slice.723), channel_id=1, source_target_pairs={{0,8},{8,16},{16,24},{24,28},{28,20},{20,12},{12,4},{4,0},{1,9},{9... | collective-permute-start | bytes 196616 | tf_op jit(solution)/shard_map/ppermute | solution.py:577
  62.0 8.0 %collective-permute-start.18 = (bf16[64,512]{1,0:T(8,128)(2,1)S(1)}, bf16[64,512]{1,0:T(8,128)(2,1)S(1)}, u32[]{:S(2)}, u32[]{:S(2)}) collective-permute-start(bf16[64,512]{1,0:T(8,128)(2,1)S(1)} %slice.724), channel_id=1, source_target_pairs={{8,0},{16,8},{24,16},{28,24},{20,28},{12,20},{4,12},{0,4},{9,1},{1... | collective-permute-start | bytes 196616 | tf_op jit(solution)/shard_map/ppermute | solution.py:577
  71.5 10.0 %collective-permute-start.5 = (bf16[128,1152]{0,1:T(8,128)(2,1)S(1)}, bf16[128,1152]{0,1:T(8,128)(2,1)S(1)}, u32[]{:S(2)}, u32[]{:S(2)}) collective-permute-start(bf16[128,1152]{0,1:T(8,128)(2,1)S(1)} %collective-permute-done.4), channel_id=1, source_target_pairs={{8,0},{16,8},{24,16},{28,24},{20,28},{12,20},{4,12},{0,4},{9,1},{1... | collective-permute-start | bytes 884744 | tf_op jit(solution)/shard_map/ppermute | solution.py:577
  73.1 7.9 %collective-permute-start.8 = (bf16[128,1152]{0,1:T(8,128)(2,1)S(1)}, bf16[128,1152]{0,1:T(8,128)(2,1)S(1)}, u32[]{:S(2)}, u32[]{:S(2)}) collective-permute-start(bf16[128,1152]{0,1:T(8,128)(2,1)S(1)} %collective-permute-done.7), channel_id=1, source_target_pairs={{0,8},{8,16},{16,24},{24,28},{28,20},{20,12},{12,4},{4,0},{1,9},{9... | collective-permute-start | bytes 884744 | tf_op jit(solution)/shard_map/ppermute | solution.py:577
  73.6 21.3 %collective-permute-start.1 = (bf16[128,2048]{1,0:T(8,128)(2,1)}, bf16[128,2048]{1,0:T(8,128)(2,1)}, u32[]{:S(2)}, u32[]{:S(2)}) collective-permute-start(bf16[128,2048]{1,0:T(8,128)(2,1)} %constant_dynamic-update-slice_fusion.8), channel_id=1, source_target_pairs={{0,1},{1,0},{2,3},{3,2},{4,5},{5,4},{6,7},{7,6},{8,9},{9,8},{10,11... | collective-permute-start | bytes 1572872 | tf_op jit(solution)/shard_map/ppermute | solution.py:645
  84.8 10.2 %collective-permute-start.2 = (bf16[128,2048]{1,0:T(8,128)(2,1)}, bf16[128,2048]{1,0:T(8,128)(2,1)}, u32[]{:S(2)}, u32[]{:S(2)}) collective-permute-start(bf16[128,2048]{1,0:T(8,128)(2,1)} %collective-permute-done), channel_id=1, source_target_pairs={{0,1},{1,0},{2,3},{3,2},{4,5},{5,4},{6,7},{7,6},{8,9},{9,8},{10,11... | collective-permute-start | bytes 1572872 | tf_op jit(solution)/shard_map/ppermute | solution.py:645
  122.1 13.6 %collective-permute-start.27 = (bf16[256,1024]{1,0:T(8,128)(2,1)S(1)}, bf16[256,1024]{1,0:T(8,128)(2,1)S(1)}, u32[]{:S(2)}, u32[]{:S(2)}) collective-permute-start(bf16[256,1024]{1,0:T(8,128)(2,1)S(1)} %slice.729), channel_id=1, source_target_pairs={{0,1},{1,0},{2,3},{3,2},{4,5},{5,4},{6,7},{7,6},{8,9},{9,8},{10,11... | collective-permute-start | bytes 1572872 | tf_op jit(solution)/shard_map/ppermute | solution.py:645
  122.3 11.3 %collective-permute-start.32 = (bf16[128,1408]{0,1:T(8,128)(2,1)S(1)}, bf16[128,1408]{0,1:T(8,128)(2,1)S(1)}, u32[]{:S(2)}, u32[]{:S(2)}) collective-permute-start(bf16[128,1408]{0,1:T(8,128)(2,1)S(1)} %constant_dynamic-update-slice_fusion.41), channel_id=1, source_target_pairs={{8,0},{16,8},{24,16},{28,24},{20,28},{12,20},{4,12},{0,4},{9,1},{1... | collective-permute-start | bytes 1081352 | tf_op jit(solution)/shard_map/ppermute | solution.py:577
  123.9 11.4 %collective-permute-start.35 = (bf16[128,1408]{0,1:T(8,128)(2,1)S(1)}, bf16[128,1408]{0,1:T(8,128)(2,1)}, u32[]{:S(2)}, u32[]{:S(2)}) collective-permute-start(bf16[128,1408]{0,1:T(8,128)(2,1)S(1)} %constant_dynamic-update-slice_fusion.41), channel_id=1, source_target_pairs={{0,8},{8,16},{16,24},{24,28},{28,20},{20,12},{12,4},{4,0},{1,9},{9... | collective-permute-start | bytes 1081352 | tf_op jit(solution)/shard_map/ppermute | solution.py:577
  124.3 19.7 %collective-permute-start.40 = (bf16[704,128]{1,0:T(8,128)(2,1)S(1)}, bf16[704,128]{1,0:T(8,128)(2,1)}, u32[]{:S(2)}, u32[]{:S(2)}) collective-permute-start(bf16[704,128]{1,0:T(8,128)(2,1)S(1)} %copy-done.33), channel_id=1, source_target_pairs={{8,0},{16,8},{24,16},{28,24},{20,28},{12,20},{4,12},{0,4},{9,1},{1... | collective-permute-start | bytes 540680 | tf_op jit(solution)/shard_map/ppermute | solution.py:577
  125.9 19.7 %collective-permute-start.43 = (bf16[704,128]{1,0:T(8,128)(2,1)S(1)}, bf16[704,128]{1,0:T(8,128)(2,1)S(1)}, u32[]{:S(2)}, u32[]{:S(2)}) collective-permute-start(bf16[704,128]{1,0:T(8,128)(2,1)S(1)} %copy-done.33), channel_id=1, source_target_pairs={{0,8},{8,16},{16,24},{24,28},{28,20},{20,12},{12,4},{4,0},{1,9},{9... | collective-permute-start | bytes 540680 | tf_op jit(solution)/shard_map/ppermute | solution.py:577
  133.5 18.4 %collective-permute-start.33 = (bf16[128,1408]{0,1:T(8,128)(2,1)S(1)}, bf16[128,1408]{0,1:T(8,128)(2,1)}, u32[]{:S(2)}, u32[]{:S(2)}) collective-permute-start(bf16[128,1408]{0,1:T(8,128)(2,1)S(1)} %collective-permute-done.32), channel_id=1, source_target_pairs={{8,0},{16,8},{24,16},{28,24},{20,28},{12,20},{4,12},{0,4},{9,1},{1... | collective-permute-start | bytes 1081352 | tf_op jit(solution)/shard_map/ppermute | solution.py:577
  135.3 18.2 %collective-permute-start.36 = (bf16[128,1408]{0,1:T(8,128)(2,1)}, bf16[128,1408]{0,1:T(8,128)(2,1)}, u32[]{:S(2)}, u32[]{:S(2)}) collective-permute-start(bf16[128,1408]{0,1:T(8,128)(2,1)} %collective-permute-done.35), channel_id=1, source_target_pairs={{0,8},{8,16},{16,24},{24,28},{28,20},{20,12},{12,4},{4,0},{1,9},{9... | collective-permute-start | bytes 1081352 | tf_op jit(solution)/shard_map/ppermute | solution.py:577
  137.6 16.3 %collective-permute-start.28 = (bf16[128,1024]{1,0:T(8,128)(2,1)}, bf16[128,1024]{1,0:T(8,128)(2,1)}, u32[]{:S(2)}, u32[]{:S(2)}) collective-permute-start(bf16[128,1024]{1,0:T(8,128)(2,1)} %slice.952), channel_id=1, source_target_pairs={{0,2},{1,3},{2,0},{3,1},{4,6},{5,7},{6,4},{7,5},{8,10},{9,11},{10,... | collective-permute-start | bytes 786440 | tf_op jit(solution)/shard_map/ppermute | solution.py:645
  149.8 8.5 %collective-permute-start.42 = (bf16[704,128]{1,0:T(8,128)(2,1)S(1)}, bf16[704,128]{1,0:T(8,128)(2,1)S(1)}, u32[]{:S(2)}, u32[]{:S(2)}) collective-permute-start(bf16[704,128]{1,0:T(8,128)(2,1)S(1)} %collective-permute-done.41), channel_id=1, source_target_pairs={{8,0},{16,8},{24,16},{28,24},{20,28},{12,20},{4,12},{0,4},{9,1},{1... | collective-permute-start | bytes 540680 | tf_op jit(solution)/shard_map/ppermute | solution.py:577
  151.4 8.5 %collective-permute-start.45 = (bf16[704,128]{1,0:T(8,128)(2,1)S(1)}, bf16[704,128]{1,0:T(8,128)(2,1)S(1)}, u32[]{:S(2)}, u32[]{:S(2)}) collective-permute-start(bf16[704,128]{1,0:T(8,128)(2,1)S(1)} %collective-permute-done.44), channel_id=1, source_target_pairs={{0,8},{8,16},{16,24},{24,28},{28,20},{20,12},{12,4},{4,0},{1,9},{9... | collective-permute-start | bytes 540680 | tf_op jit(solution)/shard_map/ppermute | solution.py:577
  151.9 15.5 %collective-permute-start.34 = (bf16[128,1408]{0,1:T(8,128)(2,1)}, bf16[128,1408]{0,1:T(8,128)(2,1)S(1)}, u32[]{:S(2)}, u32[]{:S(2)}) collective-permute-start(bf16[128,1408]{0,1:T(8,128)(2,1)} %collective-permute-done.33), channel_id=1, source_target_pairs={{8,0},{16,8},{24,16},{28,24},{20,28},{12,20},{4,12},{0,4},{9,1},{1... | collective-permute-start | bytes 1081352 | tf_op jit(solution)/shard_map/ppermute | solution.py:577
  153.5 13.5 %collective-permute-start.37 = (bf16[128,1408]{0,1:T(8,128)(2,1)}, bf16[128,1408]{0,1:T(8,128)(2,1)S(1)}, u32[]{:S(2)}, u32[]{:S(2)}) collective-permute-start(bf16[128,1408]{0,1:T(8,128)(2,1)} %collective-permute-done.36), channel_id=1, source_target_pairs={{0,8},{8,16},{16,24},{24,28},{28,20},{20,12},{12,4},{4,0},{1,9},{9... | collective-permute-start | bytes 1081352 | tf_op jit(solution)/shard_map/ppermute | solution.py:577
  156.1 9.6 %collective-permute-start.29 = (bf16[128,1024]{1,0:T(8,128)(2,1)}, bf16[128,1024]{1,0:T(8,128)(2,1)}, u32[]{:S(2)}, u32[]{:S(2)}) collective-permute-start(bf16[128,1024]{1,0:T(8,128)(2,1)} %multiply_convert_fusion.3), channel_id=1, source_target_pairs={{0,2},{1,3},{2,0},{3,1},{4,6},{5,7},{6,4},{7,5},{8,10},{9,11},{10,... | collective-permute-start | bytes 786440 | tf_op jit(solution)/shard_map/ppermute | solution.py:645
  165.7 17.7 %collective-permute-start.30 = (bf16[128,1024]{1,0:T(8,128)(2,1)}, bf16[128,1024]{1,0:T(8,128)(2,1)}, u32[]{:S(2)}, u32[]{:S(2)}) collective-permute-start(bf16[128,1024]{1,0:T(8,128)(2,1)} %multiply_convert_fusion.3), channel_id=1, source_target_pairs={{0,1},{1,0},{2,3},{3,2},{4,5},{5,4},{6,7},{7,6},{8,9},{9,8},{10,11... | collective-permute-start | bytes 786440 | tf_op jit(solution)/shard_map/ppermute | solution.py:645
  165.7 17.7 %collective-permute-start.31 = (bf16[128,1024]{1,0:T(8,128)(2,1)}, bf16[128,1024]{1,0:T(8,128)(2,1)}, u32[]{:S(2)}, u32[]{:S(2)}) collective-permute-start(bf16[128,1024]{1,0:T(8,128)(2,1)} %collective-permute-done.29), channel_id=1, source_target_pairs={{0,1},{1,0},{2,3},{3,2},{4,5},{5,4},{6,7},{7,6},{8,9},{9,8},{10,11... | collective-permute-start | bytes 786440 | tf_op jit(solution)/shard_map/ppermute | solution.py:645
  166.9 10.3 %collective-permute-start.38 = (bf16[64,1408]{0,1:T(8,128)(2,1)S(1)}, bf16[64,1408]{0,1:T(8,128)(2,1)S(1)}, u32[]{:S(2)}, u32[]{:S(2)}) collective-permute-start(bf16[64,1408]{0,1:T(8,128)(2,1)S(1)} %bitcast.95), channel_id=1, source_target_pairs={{0,8},{8,16},{16,24},{24,28},{28,20},{20,12},{12,4},{4,0},{1,9},{9... | collective-permute-start | bytes 540680 | tf_op jit(solution)/shard_map/ppermute | solution.py:577
  167.6 10.4 %collective-permute-start.39 = (bf16[64,1408]{0,1:T(8,128)(2,1)S(1)}, bf16[64,1408]{0,1:T(8,128)(2,1)}, u32[]{:S(2)}, u32[]{:S(2)}) collective-permute-start(bf16[64,1408]{0,1:T(8,128)(2,1)S(1)} %slice.734), channel_id=1, source_target_pairs={{8,0},{16,8},{24,16},{28,24},{20,28},{12,20},{4,12},{0,4},{9,1},{1... | collective-permute-start | bytes 540680 | tf_op jit(solution)/shard_map/ppermute | solution.py:577
  193.6 29.1 %collective-permute-start.50 = (bf16[256,1024]{1,0:T(8,128)(2,1)S(1)}, bf16[256,1024]{1,0:T(8,128)(2,1)S(1)}, u32[]{:S(2)}, u32[]{:S(2)}) collective-permute-start(bf16[256,1024]{1,0:T(8,128)(2,1)S(1)} %slice.745), channel_id=1, source_target_pairs={{0,1},{1,0},{2,3},{3,2},{4,5},{5,4},{6,7},{7,6},{8,9},{9,8},{10,11... | collective-permute-start | bytes 1572872 | tf_op jit(solution)/shard_map/ppermute | solution.py:645
  193.7 29.7 %collective-permute-start.48 = (bf16[256,1024]{1,0:T(8,128)(2,1)S(1)}, bf16[256,1024]{1,0:T(8,128)(2,1)S(1)}, u32[]{:S(2)}, u32[]{:S(2)}) collective-permute-start(bf16[256,1024]{1,0:T(8,128)(2,1)S(1)} %slice.740), channel_id=1, source_target_pairs={{0,1},{1,0},{2,3},{3,2},{4,5},{5,4},{6,7},{7,6},{8,9},{9,8},{10,11... | collective-permute-start | bytes 1572872 | tf_op jit(solution)/shard_map/ppermute | solution.py:645
  199.6 7.5 %collective-permute-start.91 = (bf16[64,1408]{1,0:T(8,128)(2,1)S(1)}, bf16[64,1408]{1,0:T(8,128)(2,1)S(1)}, u32[]{:S(2)}, u32[]{:S(2)}) collective-permute-start(bf16[64,1408]{1,0:T(8,128)(2,1)S(1)} %get-tuple-element.149), channel_id=1, source_target_pairs={{0,8},{8,16},{16,24},{24,28},{28,20},{20,12},{12,4},{4,0},{1,9},{9... | collective-permute-start | bytes 540680 | tf_op jit(solution)/shard_map/ppermute | solution.py:577
  200.1 8.6 %collective-permute-start.95 = (bf16[64,1408]{1,0:T(8,128)(2,1)S(1)}, bf16[64,1408]{1,0:T(8,128)(2,1)S(1)}, u32[]{:S(2)}, u32[]{:S(2)}) collective-permute-start(bf16[64,1408]{1,0:T(8,128)(2,1)S(1)} %get-tuple-element.150), channel_id=1, source_target_pairs={{8,0},{16,8},{24,16},{28,24},{20,28},{12,20},{4,12},{0,4},{9,1},{1... | collective-permute-start | bytes 540680 | tf_op jit(solution)/shard_map/ppermute | solution.py:577
  201.7 8.8 %collective-permute-start.100 = (bf16[704,128]{1,0:T(8,128)(2,1)S(1)}, bf16[704,128]{1,0:T(8,128)(2,1)S(1)}, u32[]{:S(2)}, u32[]{:S(2)}) collective-permute-start(bf16[704,128]{1,0:T(8,128)(2,1)S(1)} %pad_maximum_fusion.10), channel_id=1, source_target_pairs={{0,8},{8,16},{16,24},{24,28},{28,20},{20,12},{12,4},{4,0},{1,9},{9... | collective-permute-start | bytes 540680 | tf_op jit(solution)/shard_map/ppermute | solution.py:577
  208.8 16.1 %collective-permute-start.92 = (bf16[128,1408]{1,0:T(8,128)(2,1)S(1)}, bf16[128,1408]{1,0:T(8,128)(2,1)S(1)}, u32[]{:S(2)}, u32[]{:S(2)}) collective-permute-start(bf16[128,1408]{1,0:T(8,128)(2,1)S(1)} %pad_maximum_fusion.6), channel_id=1, source_target_pairs={{0,8},{8,16},{16,24},{24,28},{28,20},{20,12},{12,4},{4,0},{1,9},{9... | collective-permute-start | bytes 1081352 | tf_op jit(solution)/shard_map/ppermute | solution.py:577
  210.7 10.3 %collective-permute-start.101 = (bf16[704,128]{1,0:T(8,128)(2,1)S(1)}, bf16[704,128]{1,0:T(8,128)(2,1)S(1)}, u32[]{:S(2)}, u32[]{:S(2)}) collective-permute-start(bf16[704,128]{1,0:T(8,128)(2,1)S(1)} %add_convert_fusion.11), channel_id=1, source_target_pairs={{0,8},{8,16},{16,24},{24,28},{28,20},{20,12},{12,4},{4,0},{1,9},{9... | collective-permute-start | bytes 540680 | tf_op jit(solution)/shard_map/ppermute | solution.py:577
  213.9 23.0 %collective-permute-start.96 = (bf16[128,1408]{1,0:T(8,128)(2,1)S(1)}, bf16[128,1408]{1,0:T(8,128)(2,1)S(1)}, u32[]{:S(2)}, u32[]{:S(2)}) collective-permute-start(bf16[128,1408]{1,0:T(8,128)(2,1)S(1)} %pad_maximum_fusion.7), channel_id=1, source_target_pairs={{8,0},{16,8},{24,16},{28,24},{20,28},{12,20},{4,12},{0,4},{9,1},{1... | collective-permute-start | bytes 1081352 | tf_op jit(solution)/shard_map/ppermute | solution.py:577
  222.7 17.2 %collective-permute-start.102 = (bf16[704,128]{1,0:T(8,128)(2,1)S(1)}, bf16[704,128]{1,0:T(8,128)(2,1)S(1)}, u32[]{:S(2)}, u32[]{:S(2)}) collective-permute-start(bf16[704,128]{1,0:T(8,128)(2,1)S(1)} %get-tuple-element.166), channel_id=1, source_target_pairs={{0,8},{8,16},{16,24},{24,28},{28,20},{20,12},{12,4},{4,0},{1,9},{9... | collective-permute-start | bytes 540680 | tf_op jit(solution)/shard_map/ppermute | solution.py:577
  223.4 7.6 %collective-permute-start.51 = (bf16[128,1024]{1,0:T(8,128)(2,1)S(1)}, bf16[128,1024]{1,0:T(8,128)(2,1)S(1)}, u32[]{:S(2)}, u32[]{:S(2)}) collective-permute-start(bf16[128,1024]{1,0:T(8,128)(2,1)S(1)} %slice.950), channel_id=1, source_target_pairs={{0,2},{1,3},{2,0},{3,1},{4,6},{5,7},{6,4},{7,5},{8,10},{9,11},{10,... | collective-permute-start | bytes 786440 | tf_op jit(solution)/shard_map/ppermute | solution.py:645
  224.9 9.5 %collective-permute-start.49 = (bf16[128,1024]{1,0:T(8,128)(2,1)S(1)}, bf16[128,1024]{1,0:T(8,128)(2,1)S(1)}, u32[]{:S(2)}, u32[]{:S(2)}) collective-permute-start(bf16[128,1024]{1,0:T(8,128)(2,1)S(1)} %slice.951), channel_id=1, source_target_pairs={{0,2},{1,3},{2,0},{3,1},{4,6},{5,7},{6,4},{7,5},{8,10},{9,11},{10,... | collective-permute-start | bytes 786440 | tf_op jit(solution)/shard_map/ppermute | solution.py:645
  226.6 10.4 %collective-permute-start.93 = (bf16[128,1408]{1,0:T(8,128)(2,1)S(1)}, bf16[128,1408]{1,0:T(8,128)(2,1)S(1)}, u32[]{:S(2)}, u32[]{:S(2)}) collective-permute-start(bf16[128,1408]{1,0:T(8,128)(2,1)S(1)} %add_convert_fusion.3), channel_id=1, source_target_pairs={{0,8},{8,16},{16,24},{24,28},{28,20},{20,12},{12,4},{4,0},{1,9},{9... | collective-permute-start | bytes 1081352 | tf_op jit(solution)/shard_map/ppermute | solution.py:577
  231.0 8.9 %collective-permute-start.106 = (bf16[704,128]{1,0:T(8,128)(2,1)S(1)}, bf16[704,128]{1,0:T(8,128)(2,1)S(1)}, u32[]{:S(2)}, u32[]{:S(2)}) collective-permute-start(bf16[704,128]{1,0:T(8,128)(2,1)S(1)} %add_convert_fusion.8), channel_id=1, source_target_pairs={{8,0},{16,8},{24,16},{28,24},{20,28},{12,20},{4,12},{0,4},{9,1},{1... | collective-permute-start | bytes 540680 | tf_op jit(solution)/shard_map/ppermute | solution.py:577
  237.0 14.5 %collective-permute-start.53 = (bf16[128,1024]{1,0:T(8,128)(2,1)S(1)}, bf16[128,1024]{1,0:T(8,128)(2,1)S(1)}, u32[]{:S(2)}, u32[]{:S(2)}) collective-permute-start(bf16[128,1024]{1,0:T(8,128)(2,1)S(1)} %get-tuple-element.139), channel_id=1, source_target_pairs={{0,1},{1,0},{2,3},{3,2},{4,5},{5,4},{6,7},{7,6},{8,9},{9,8},{10,11... | collective-permute-start | bytes 786440 | tf_op jit(solution)/shard_map/ppermute | solution.py:645
  238.0 11.0 %collective-permute-start.97 = (bf16[128,1408]{1,0:T(8,128)(2,1)S(1)}, bf16[128,1408]{1,0:T(8,128)(2,1)S(1)}, u32[]{:S(2)}, u32[]{:S(2)}) collective-permute-start(bf16[128,1408]{1,0:T(8,128)(2,1)S(1)} %get-tuple-element.146), channel_id=1, source_target_pairs={{8,0},{16,8},{24,16},{28,24},{20,28},{12,20},{4,12},{0,4},{9,1},{1... | collective-permute-start | bytes 1081352 | tf_op jit(solution)/shard_map/ppermute | solution.py:577
  240.8 107.7 %collective-permute-start.94 = (bf16[128,1408]{1,0:T(8,128)(2,1)}, bf16[128,1408]{1,0:T(8,128)(2,1)}, u32[]{:S(2)}, u32[]{:S(2)}) collective-permute-start(bf16[128,1408]{1,0:T(8,128)(2,1)} %get-tuple-element.145), channel_id=1, source_target_pairs={{0,8},{8,16},{16,24},{24,28},{28,20},{20,12},{12,4},{4,0},{1,9},{9... | collective-permute-start | bytes 1081352 | tf_op jit(solution)/shard_map/ppermute | solution.py:577
  241.9 9.6 %collective-permute-start.54 = (bf16[128,1024]{1,0:T(8,128)(2,1)S(1)}, bf16[128,1024]{1,0:T(8,128)(2,1)S(1)}, u32[]{:S(2)}, u32[]{:S(2)}) collective-permute-start(bf16[128,1024]{1,0:T(8,128)(2,1)S(1)} %collective-permute-done.52), channel_id=1, source_target_pairs={{0,1},{1,0},{2,3},{3,2},{4,5},{5,4},{6,7},{7,6},{8,9},{9,8},{10,11... | collective-permute-start | bytes 786440 | tf_op jit(solution)/shard_map/ppermute | solution.py:645
  249.8 98.9 %collective-permute-start.98 = (bf16[128,1408]{1,0:T(8,128)(2,1)}, bf16[128,1408]{1,0:T(8,128)(2,1)}, u32[]{:S(2)}, u32[]{:S(2)}) collective-permute-start(bf16[128,1408]{1,0:T(8,128)(2,1)} %add_convert_fusion), channel_id=1, source_target_pairs={{8,0},{16,8},{24,16},{28,24},{20,28},{12,20},{4,12},{0,4},{9,1},{1... | collective-permute-start | bytes 1081352 | tf_op jit(solution)/shard_map/ppermute | solution.py:577
  282.7 89.5 %collective-permute-start.55 = (bf16[256,1024]{1,0:T(8,128)(2,1)}, bf16[256,1024]{1,0:T(8,128)(2,1)}, u32[]{:S(2)}, u32[]{:S(2)}) collective-permute-start(bf16[256,1024]{1,0:T(8,128)(2,1)} %slice.749), channel_id=1, source_target_pairs={{0,1},{1,0},{2,3},{3,2},{4,5},{5,4},{6,7},{7,6},{8,9},{9,8},{10,11... | collective-permute-start | bytes 1572872 | tf_op jit(solution)/shard_map/ppermute | solution.py:645
  284.7 19.6 %collective-permute-start.75 = (bf16[64,512]{1,0:T(8,128)(2,1)}, bf16[64,512]{1,0:T(8,128)(2,1)}, u32[]{:S(2)}, u32[]{:S(2)}) collective-permute-start(bf16[64,512]{1,0:T(8,128)(2,1)} %get-tuple-element.186), channel_id=1, source_target_pairs={{0,8},{8,16},{16,24},{24,28},{28,20},{20,12},{12,4},{4,0},{1,9},{9... | collective-permute-start | bytes 196616 | tf_op jit(solution)/shard_map/ppermute | solution.py:577
  311.4 11.0 %collective-permute-start.67 = (bf16[64,1024]{1,0:T(8,128)(2,1)S(1)}, bf16[64,1024]{1,0:T(8,128)(2,1)S(1)}, u32[]{:S(2)}, u32[]{:S(2)}) collective-permute-start(bf16[64,1024]{1,0:T(8,128)(2,1)S(1)} %copy-done.43), channel_id=1, source_target_pairs={{0,8},{8,16},{16,24},{24,28},{28,20},{20,12},{12,4},{4,0},{1,9},{9... | collective-permute-start | bytes 393224 | tf_op jit(solution)/shard_map/ppermute | solution.py:577
  341.9 12.1 %collective-permute-start.80 = (bf16[128,512]{1,0:T(8,128)(2,1)}, bf16[128,512]{1,0:T(8,128)(2,1)}, u32[]{:S(2)}, u32[]{:S(2)}) collective-permute-start(bf16[128,512]{1,0:T(8,128)(2,1)} %pad_maximum_fusion.17), channel_id=1, source_target_pairs={{8,0},{16,8},{24,16},{28,24},{20,28},{12,20},{4,12},{0,4},{9,1},{1... | collective-permute-start | bytes 393224 | tf_op jit(solution)/shard_map/ppermute | solution.py:577
  343.7 16.3 %collective-permute-start.88 = (bf16[512,128]{1,0:T(8,128)(2,1)}, bf16[512,128]{1,0:T(8,128)(2,1)}, u32[]{:S(2)}, u32[]{:S(2)}) collective-permute-start(bf16[512,128]{1,0:T(8,128)(2,1)} %pad_maximum_fusion.19), channel_id=1, source_target_pairs={{8,0},{16,8},{24,16},{28,24},{20,28},{12,20},{4,12},{0,4},{9,1},{1... | collective-permute-start | bytes 393224 | tf_op jit(solution)/shard_map/ppermute | solution.py:577
  348.5 16.4 %collective-permute-start.68 = (bf16[128,1024]{1,0:T(8,128)(2,1)}, bf16[128,1024]{1,0:T(8,128)(2,1)S(1)}, u32[]{:S(2)}, u32[]{:S(2)}) collective-permute-start(bf16[128,1024]{1,0:T(8,128)(2,1)} %pad_maximum_fusion.8), channel_id=1, source_target_pairs={{0,8},{8,16},{16,24},{24,28},{28,20},{20,12},{12,4},{4,0},{1,9},{9... | collective-permute-start | bytes 786440 | tf_op jit(solution)/shard_map/ppermute | solution.py:577
  348.7 10.1 %collective-permute-start.77 = (bf16[128,512]{1,0:T(8,128)(2,1)}, bf16[128,512]{1,0:T(8,128)(2,1)}, u32[]{:S(2)}, u32[]{:S(2)}) collective-permute-start(bf16[128,512]{1,0:T(8,128)(2,1)} %add_convert_fusion.21), channel_id=1, source_target_pairs={{0,8},{8,16},{16,24},{24,28},{28,20},{20,12},{12,4},{4,0},{1,9},{9... | collective-permute-start | bytes 393224 | tf_op jit(solution)/shard_map/ppermute | solution.py:577
  354.0 28.8 %collective-permute-start.72 = (bf16[128,1024]{1,0:T(8,128)(2,1)}, bf16[128,1024]{1,0:T(8,128)(2,1)S(1)}, u32[]{:S(2)}, u32[]{:S(2)}) collective-permute-start(bf16[128,1024]{1,0:T(8,128)(2,1)} %pad_maximum_fusion.9), channel_id=1, source_target_pairs={{8,0},{16,8},{24,16},{28,24},{20,28},{12,20},{4,12},{0,4},{9,1},{1... | collective-permute-start | bytes 786440 | tf_op jit(solution)/shard_map/ppermute | solution.py:577
  363.8 11.8 %collective-permute-start.78 = (bf16[128,512]{1,0:T(8,128)(2,1)S(1)}, bf16[128,512]{1,0:T(8,128)(2,1)S(1)}, u32[]{:S(2)}, u32[]{:S(2)}) collective-permute-start(bf16[128,512]{1,0:T(8,128)(2,1)S(1)} %get-tuple-element.182), channel_id=1, source_target_pairs={{0,8},{8,16},{16,24},{24,28},{28,20},{20,12},{12,4},{4,0},{1,9},{9... | collective-permute-start | bytes 393224 | tf_op jit(solution)/shard_map/ppermute | solution.py:577
  367.1 14.1 %collective-permute-start.86 = (bf16[512,128]{1,0:T(8,128)(2,1)S(1)}, bf16[512,128]{1,0:T(8,128)(2,1)S(1)}, u32[]{:S(2)}, u32[]{:S(2)}) collective-permute-start(bf16[512,128]{1,0:T(8,128)(2,1)S(1)} %get-tuple-element.174), channel_id=1, source_target_pairs={{0,8},{8,16},{16,24},{24,28},{28,20},{20,12},{12,4},{4,0},{1,9},{9... | collective-permute-start | bytes 393224 | tf_op jit(solution)/shard_map/ppermute | solution.py:577
  371.3 11.5 %collective-permute-start.69 = (bf16[128,1024]{1,0:T(8,128)(2,1)S(1)}, bf16[128,1024]{1,0:T(8,128)(2,1)S(1)}, u32[]{:S(2)}, u32[]{:S(2)}) collective-permute-start(bf16[128,1024]{1,0:T(8,128)(2,1)S(1)} %add_convert_fusion.7), channel_id=1, source_target_pairs={{0,8},{8,16},{16,24},{24,28},{28,20},{20,12},{12,4},{4,0},{1,9},{9... | collective-permute-start | bytes 786440 | tf_op jit(solution)/shard_map/ppermute | solution.py:577
  (98 other events, 1105.3 us)
